TPU v7x, 1024 devices: a whole 4x4x32 slice. The times are simulated.
1024 devices in a mesh: dp: 16 (over x, y), seq: 64 (over z, core).
Axes of the slice: x: 4, y: 4, z: 32, core: 2. Of those that a mesh axis runs over, the one named last changes fastest.
Arguments:
- section_input: bfloat16 [16, 32768, 384], P('dp', 'seq'), may hold values from -42 to 42
- kernel: bfloat16 [384, 5, 384], P('seq'), may hold values from -0.125 to 0.125
- cotangent: bfloat16 [16, 32768, 384], P('dp', 'seq'), may hold values from -16 to 16
Outputs:
- block_output: bfloat16 [16, 32768, 384], P('dp', 'seq')
- input_grad: bfloat16 [16, 32768, 384], P('dp', 'seq')
- kernel_grad: float32 [384, 5, 384], P('seq')
All inputs are finite; a program needn't handle non-finite values.
Results may differ from a plain program's by a relative error of at most 0.0065.
Values may be sent and summed in bfloat16 or wider, within the bound.
No kernel may reach another device: no remote copies, remote signals or barrier semaphores. Data moves between devices by JAX's collectives and lax.ppermute only.
A program may use at most 32 MiB of HBM per device.

v0:
```python
import jax
import jax.numpy as jnp
from jax import lax
from jax.sharding import PartitionSpec as P


def padded(cells, sides, width):
    for axis, dim in sides:
        count = lax.axis_size(axis)
        ends = count - 1
        head = lax.slice_in_dim(cells, 0, width, axis=dim)
        tail = lax.slice_in_dim(cells, cells.shape[dim] - width, cells.shape[dim], axis=dim)
        cells = jnp.concatenate(
            [
                lax.ppermute(tail, axis, [(i, (i + 1) % count) for i in range(ends)]),
                cells,
                lax.ppermute(head, axis, [((i + 1) % count, i) for i in range(ends)]),
            ],
            axis=dim,
        )
    return cells


def gelu_value(values):
    return 0.5 * values * (1.0 + jax.scipy.special.erf(values * 0.7071067811865476))


def gelu_slope(values):
    cumulative = 0.5 * (1.0 + jax.scipy.special.erf(values * 0.7071067811865476))
    return cumulative + values * jnp.exp(-0.5 * values * values) * 0.3989422804014327


def local(section_input, kernel, cotangent):
    tap_count = kernel.shape[1]
    half_width = (tap_count - 1) // 2
    inputs = section_input[0].astype(jnp.float32)
    out_grad = cotangent[0]
    length = inputs.shape[0]
    width = inputs.shape[1]
    scale = jnp.sqrt(jnp.mean(inputs * inputs, axis=-1, keepdims=True) + 1e-05)
    normed = inputs / scale
    act = gelu_value(normed).astype(jnp.bfloat16)
    rimmed = padded(jnp.stack([act, out_grad]), (("seq", 1),), half_width)
    act_pad = rimmed[0]
    grad_pad = rimmed[1]
    empty = jnp.zeros((length, width), jnp.float32)
    piece = lax.all_gather(kernel, "seq", axis=0, tiled=True)
    total = jnp.zeros((length, piece.shape[0]), jnp.float32)
    for shift in range(tap_count):
        total = total + lax.dot_general(
            act_pad[shift : shift + length],
            piece[:, shift, :],
            (((1,), (1,)), ((), ())),
            preferred_element_type=jnp.float32,
        )
    branch = total.astype(jnp.bfloat16)
    carry = empty
    piece = lax.all_gather(kernel, "seq", axis=0, tiled=True)
    grad_cols = grad_pad
    for shift in range(tap_count):
        begin = 2 * half_width - shift
        carry = carry + jnp.dot(
            grad_cols[begin : begin + length],
            piece[:, shift, :],
            preferred_element_type=jnp.float32,
        )
    block_output = (inputs + branch.astype(jnp.float32)).astype(jnp.bfloat16)
    grad_cols = out_grad
    pieces = []
    for shift in range(tap_count):
        pieces.append(
            lax.dot_general(
                grad_cols,
                act_pad[shift : shift + length],
                (((0,), (0,)), ((), ())),
                preferred_element_type=jnp.float32,
            )
        )
    partial_grad = lax.psum_scatter(
        jnp.stack(pieces, axis=1), "seq", scatter_dimension=0, tiled=True
    )
    summed = lax.psum(partial_grad, "dp")
    kernel_grad = summed / (lax.axis_size("dp") * section_input.shape[0])
    normed_grad = carry * gelu_slope(normed)
    project = jnp.mean(normed_grad * normed, axis=-1, keepdims=True)
    input_grad = (out_grad.astype(jnp.float32) + (normed_grad - normed * project) / scale).astype(
        jnp.bfloat16
    )
    return (block_output[None], input_grad[None], kernel_grad)


def solution(mesh):
    return jax.shard_map(
        local,
        mesh=mesh,
        in_specs=(P("dp", "seq", None), P("seq", None, None), P("dp", "seq", None)),
        out_specs=(P("dp", "seq", None), P("dp", "seq", None), P("seq", None, None)),
        check_vma=False,
    )
```

profile of v0, /device:TPU:32, one launch (start us, length us, event | category | flops | bytes accessed | tf_op | source)
XLA Modules:
  0.0 446.9 jit_solution(17849107955575348222)
XLA Ops:
  7.2 0.0 copy-start
  7.2 0.0 all-gather.2.cloned.1.call-start
  7.2 1.4 copy.20
  8.6 0.0 all-gather.2.cloned.1.call-update
  8.7 0.0 reduce-scatter.2.cloned.1.call-start
  8.7 1.1 fusion.13
  9.9 1.3 multiply_convert_fusion
  11.2 0.7 pad_maximum_fusion.1
  11.9 1.9 collective-permute-start.1
  13.8 2.4 collective-permute-start
  16.2 0.0 collective-permute-done.1
  16.2 13.6 %collective-permute-done = bf16[2,2,384]{2,1,0:T(2,128)(2,1)S(1)} collective-permute-done((bf16[2,2,384]{2,1,0:T(2,128)(2,1)S(1)}, bf16[2,2,384]{2,1,0:T(2,128)(2,1)S(1)}, u32[]{:S(2)}, u32[]{:S(2)}) %collective-permute-start) | collective-permute-done | bytes 3104 | tf_op jit(solution)/shard_map/ppermute | solution.py:15
  29.9 1.4 pad_maximum_fusion
  31.3 0.0 copy-done
  31.3 1.2 fusion.9
  32.5 1.3 fusion.8
  33.8 1.2 fusion.7
  35.0 1.2 fusion.6
  36.2 1.2 fusion.5
  37.5 5.3 %copy.31 = f32[384,5,384]{2,1,0:T(8,128)} copy(f32[384,5,384]{0,2,1:T(8,128)} %fusion.5) | data formatting | bytes 5898240 | tf_op jit(solution)/shard_map/stack | solution.py:80
  42.8 0.0 reduce-scatter.2.cloned.1.call-update
  42.8 112.3 %all-gather.2.cloned.1.call-done = bf16[384,5,384]{2,1,0:T(8,128)(2,1)} async-done(((bf16[6,5,384]{2,1,0:T(8,128)(2,1)}), bf16[384,5,384]{2,1,0:T(8,128)(2,1)}) %all-gather.2.cloned.1.call-update) | async-done | bytes 1474576 | tf_op jit(solution)/shard_map/all_gather | solution.py:47
  155.1 8.6 %fusion.29 = (bf16[384,1,384]{2,1,0:T(2,128)(2,1)S(1)}, bf16[384,1,384]{2,1,0:T(2,128)(2,1)S(1)}, bf16[384,1,384]{2,1,0:T(2,128)(2,1)S(1)}, bf16[384,1,384]{2,1,0:T(2,128)(2,1)S(1)}, bf16[384,1,384]{2,1,0:T(2,128)(2,1)S(1)}) fusion(bf16[384,5,384]{2,1,0:T(8,128)(2,1)} %all-gather.2.cloned.1.call-done), kind=kLoop, calls=%fused_computation.68 | loop fusion | bytes 2949120 | tf_op jit(solution)/shard_map/slice | solution.py:52
  163.7 0.4 fusion.28
  164.1 0.0 copy-start.1
  164.1 0.4 convolution_add_fusion.7
  164.6 0.4 convolution_add_fusion.6
  165.0 0.4 convolution_add_fusion.5
  165.4 0.0 copy-done.1
  165.4 1.2 fusion.10
  166.6 0.4 fusion.18
  167.0 0.4 convolution_add_fusion.3
  167.4 0.4 convolution_add_fusion.2
  167.8 0.4 convolution_add_fusion.1
  168.2 0.7 multiply_reduce_fusion
  169.0 1.1 fusion.27
  170.0 193.7 %reduce-scatter.2.cloned.1.call-done = f32[6,5,384]{2,1,0:T(8,128)} async-done(((f32[384,5,384]{2,1,0:T(8,128)}), f32[6,5,384]{2,1,0:T(8,128)}) %reduce-scatter.2.cloned.1.call-update) | async-done | bytes 46096 | tf_op jit(solution)/shard_map/reduce_scatter | solution.py:79
  363.8 75.7 %psum.7 = f32[6,5,384]{2,1,0:T(8,128)S(1)} all-reduce(f32[6,5,384]{2,1,0:T(8,128)} %reduce-scatter.2.cloned.1.call-done), channel_id=1, replica_groups=mesh['dp'=16,'seq'=64] {'dp'}, use_global_device_ids=true, to_apply=%region_3.0 | all-reduce | flops 11520 | bytes 92160 | tf_op jit(solution)/shard_map/psum | solution.py:82
  439.4 0.6 copy.32
  (3 shorter events, 0.0 us)
Async XLA Ops:
  7.2 24.1 %copy-start = (bf16[1,512,384]{2,1,0:T(8,128)(2,1)S(1)}, bf16[1,512,384]{2,1,0:T(8,128)(2,1)}, u32[]{:S(2)}) copy-start(bf16[1,512,384]{2,1,0:T(8,128)(2,1)} %param.5) | copy-start | bytes 1179652
  7.2 147.9 %all-gather.2.cloned.1.call-start = ((), (), s32[]{:S(2)}) async-start(), calls=%async_computation.1 | async-start | bytes 2396160 | tf_op jit(solution)/shard_map/all_gather | solution.py:47
  8.7 355.1 %reduce-scatter.2.cloned.1.call-start = ((), (), s32[]{:S(2)}) async-start(), calls=%async_computation.2 | async-start | bytes 4792320 | tf_op jit(solution)/shard_map/reduce_scatter | solution.py:79
  11.9 4.3 collective-permute-start.1
  13.8 16.0 %collective-permute-start = (bf16[2,2,384]{2,1,0:T(2,128)(2,1)S(1)}, bf16[2,2,384]{2,1,0:T(2,128)(2,1)S(1)}, u32[]{:S(2)}, u32[]{:S(2)}) collective-permute-start(bf16[2,2,384]{2,1,0:T(2,128)(2,1)S(1)} %get-tuple-element.20), channel_id=1, source_target_pairs={{0,1},{1,2},{2,3},{3,4},{4,5},{5,6},{6,7},{7,8},{8,9},{9,10},{10,1... | collective-permute-start | bytes 9224 | tf_op jit(solution)/shard_map/ppermute | solution.py:15
  164.1 1.3 copy-start.1
Sparse Core Ops, SparseCore 0:
  11.3 143.7 all-gather.1
  158.5 205.2 reduce-scatter.1
where the time goes:
time: 447 us
  waiting for transfers between devices  320 us (72%)
  blocking collectives  75.7 us (17%)
  local copies, waits for them, and re-layouts  16 us (4%)
  between operations  14.2 us (3%)
  matrix products  11.4 us (3%)
  other arithmetic  5.68 us (1%)
    reduce_scatter x1, waiting for transfers between devices, local(): lax.psum_scatter(jnp.stack(pieces, axis=1), 'seq', scatter_dimension=0, t...  194 us
    all_gather x1, waiting for transfers between devices, local(): piece = lax.all_gather(kernel, 'seq', axis=0, tiled=True)  112 us
    psum x1, blocking collectives, local(): summed = lax.psum(partial_grad, 'dp')  75.7 us
    ppermute x1, waiting for transfers between devices, padded(): lax.ppermute(tail, axis, [(i, (i + 1) % count) for i in range(ends)])  13.6 us
  transfers between devices with their start and end apart: 4, of which 3 were waited for; matrix products, arithmetic and copies ran while one was open for 7% of the time, Pallas kernels for 0%

commit v1 on v0

v1 whole, which is shorter than its diff:
```python
import jax
import jax.numpy as jnp
from jax import lax
from jax.sharding import Mesh, PartitionSpec as P

XY = ("x", "y")
SEQ = ("z", "core")
BF = jnp.bfloat16
F32 = jnp.float32


def gelu_value(values):
    return 0.5 * values * (1.0 + jax.scipy.special.erf(values * 0.7071067811865476))


def gelu_slope(values):
    cumulative = 0.5 * (1.0 + jax.scipy.special.erf(values * 0.7071067811865476))
    return cumulative + values * jnp.exp(-0.5 * values * values) * 0.3989422804014327


def norm(rows):
    inputs = rows.astype(F32)
    scale = jnp.sqrt(jnp.mean(inputs * inputs, axis=-1, keepdims=True) + 1e-05)
    return inputs, scale, inputs / scale


def order_matrix(width, depth, core):
    half, rest = width // 2, width // (4 * depth)
    j = lax.broadcasted_iota(jnp.int32, (width, width), 1)
    o = lax.broadcasted_iota(jnp.int32, (width, width), 0)
    side = j // half
    within = j % half
    pair = within // (2 * depth)
    place = (within // 2) % depth
    member = j % 2
    source = (place * 2 + (side + core) % 2) * (2 * rest) + 2 * pair + member
    return (o == source).astype(BF)


def local(section_input, kernel, cotangent):
    rows_in = section_input[0]
    out_grad = cotangent[0]
    length, width = rows_in.shape
    held, taps, _ = kernel.shape
    edge = (taps - 1) // 2
    depth = lax.axis_size("z")
    groups = lax.axis_size(XY)
    count = lax.axis_size(SEQ)
    pairs = held // 2
    blocks = taps * pairs
    half = width // 2
    core = lax.axis_index("core")
    spot = lax.axis_index(XY)

    by_block = kernel.reshape(pairs, 2, taps, width).transpose(2, 0, 1, 3).reshape(blocks, 2, width)
    mine = lax.dynamic_index_in_dim(by_block, jnp.minimum(spot, blocks - 1), 0, keepdims=False)
    along_z = lax.all_to_all(jnp.broadcast_to(mine, (depth, 2, width)), "z", 0, 0)
    along_z = along_z.reshape(2 * depth, width)
    own_half = lax.all_to_all(jnp.broadcast_to(along_z, (groups, 2 * depth, width)), XY, 0, 0)
    own_half = own_half[:blocks].reshape(taps, half, width)
    swap = [(0, 1), (1, 0)]
    other_half = lax.ppermute(own_half, "core", swap)
    weights = jnp.concatenate([own_half, other_half], axis=1)

    both = jnp.stack([rows_in, out_grad])
    before = lax.ppermute(both[:, length - edge :], SEQ, [(i, i + 1) for i in range(count - 1)])
    after = lax.ppermute(both[:, :edge], SEQ, [(i + 1, i) for i in range(count - 1)])
    padded_in = jnp.concatenate([before[0], rows_in, after[0]], axis=0)
    padded_grad = jnp.concatenate([before[1], out_grad, after[1]], axis=0)
    inputs, scale, normed = norm(padded_in)
    act = gelu_value(normed).astype(BF)
    inputs, scale, normed = (v[edge : edge + length] for v in (inputs, scale, normed))
    order = order_matrix(width, depth, core)
    grouped = jnp.dot(padded_grad, order, preferred_element_type=F32).astype(BF)

    centre = grouped[edge : edge + length]
    parts = jnp.stack(
        [
            lax.dot_general(
                centre,
                act[shift : shift + length],
                (((0,), (0,)), ((), ())),
                preferred_element_type=F32,
            )
            for shift in range(taps)
        ]
    )
    got = lax.ppermute(parts[:, half:].astype(BF), "core", swap)
    chip = (parts[:, :half] + got.astype(F32)).astype(BF).reshape(blocks, 2 * depth, width)
    chip = jnp.pad(chip, ((0, groups - blocks), (0, 0), (0, 0)))
    plane = lax.all_to_all(chip, XY, 0, 0)
    plane = sum(plane[i].astype(F32) for i in range(groups)).astype(BF).reshape(depth, 2, width)
    line = lax.all_to_all(plane, "z", 0, 0)
    line = jnp.sum(line.astype(F32), axis=0) / (groups * section_input.shape[0])
    full = lax.all_to_all(jnp.broadcast_to(line, (groups, 2, width)), XY, 0, 0)
    kernel_grad = (
        full[:blocks].reshape(taps, pairs, 2, width).transpose(1, 2, 0, 3).reshape(held, taps, width)
    )

    total = jnp.zeros((length, width), F32)
    carry = jnp.zeros((length, width), F32)
    for shift in range(taps):
        total = total + lax.dot_general(
            act[shift : shift + length],
            weights[shift],
            (((1,), (1,)), ((), ())),
            preferred_element_type=F32,
        )
        begin = 2 * edge - shift
        carry = carry + jnp.dot(
            grouped[begin : begin + length], weights[shift], preferred_element_type=F32
        )
    branch = lax.dot_general(
        total.astype(BF), order, (((1,), (1,)), ((), ())), preferred_element_type=F32
    )
    block_output = (inputs + branch).astype(BF)
    normed_grad = carry * gelu_slope(normed)
    project = jnp.mean(normed_grad * normed, axis=-1, keepdims=True)
    input_grad = (out_grad.astype(F32) + (normed_grad - normed * project) / scale).astype(BF)
    return (block_output[None], input_grad[None], kernel_grad)


def solution(mesh):
    seq = mesh.shape["seq"]
    side = int(round(mesh.shape["dp"] ** 0.5))
    fine = Mesh(mesh.devices.reshape(side, side, seq // 2, 2), XY + SEQ)
    return jax.shard_map(
        local,
        mesh=fine,
        in_specs=(P(XY, SEQ, None), P(SEQ, None, None), P(XY, SEQ, None)),
        out_specs=(P(XY, SEQ, None), P(XY, SEQ, None), P(SEQ, None, None)),
        check_vma=False,
    )
```

time: 447 us -> 150 us (0.34)
  the two profiles are of different devices: /device:TPU:32 before, /device:TPU:2 now
where the time goes in v1:
time: 150 us; the launch traced here: 149 us
  starting transfers between devices  76.8 us (51%)
  waiting for transfers between devices  33.9 us (23%)
  matrix products  20.1 us (13%)
  local copies, waits for them, and re-layouts  8.99 us (6%)
  other arithmetic  8.24 us (5%)
    all_to_all x1, starting transfers between devices, local(): lax.all_to_all(jnp.broadcast_to(mine, (depth, 2, width)), 'z', 0, 0)  28.7 us
    all_to_all x1, starting transfers between devices, local(): line = lax.all_to_all(plane, 'z', 0, 0)  19.2 us
    dot_general x5, matrix products, local(): jnp.dot(grouped[begin:begin + length], weights[shift], preferred_element_...  8.69 us
    all_to_all x1, starting transfers between devices, local(): lax.all_to_all(jnp.broadcast_to(along_z, (groups, 2 * depth, width)), XY,...  7.48 us
    all_to_all x1, waiting for transfers between devices, local(): lax.all_to_all(jnp.broadcast_to(along_z, (groups, 2 * depth, width)), XY,...  7.22 us
    all_to_all x1, waiting for transfers between devices, local(): lax.all_to_all(jnp.broadcast_to(mine, (depth, 2, width)), 'z', 0, 0)  6.42 us
    all_to_all x1, starting transfers between devices, local(): plane = lax.all_to_all(chip, XY, 0, 0)  6.37 us
    all_to_all x1, waiting for transfers between devices, local(): plane = lax.all_to_all(chip, XY, 0, 0)  6.36 us
  transfers between devices with their start and end apart: 9, of which 6 were waited for; matrix products, arithmetic and copies ran while one was open for 22% of the time, Pallas kernels for 0%

profile of v1, /device:TPU:2, one launch (start us, length us, event | category | flops | bytes accessed | tf_op | source)
XLA Modules:
  0.0 149.0 jit_solution(4339140463674610133)
XLA Ops:
  0.6 0.0 copy-start
  0.7 0.8 reshape.102
  1.5 0.6 broadcast_in_dim.17
  2.2 28.7 %all-to-all-start = ((bf16[32,2,384]{2,1,0:T(2,128)(2,1)}), bf16[32,2,384]{2,1,0:T(2,128)(2,1)S(1)}, u32[]{:S(2)}, u32[]{:S(2)}) async-start(bf16[32,2,384]{2,1,0:T(2,128)(2,1)} %broadcast_in_dim.17), calls=%async_computation | async-start | bytes 98304 | tf_op jit(solution)/shard_map/all_to_all | solution.py:57
  30.9 1.0 constant_dynamic-update-slice_fusion.1
  31.9 0.0 copy-start.2
  32.0 1.1 constant_dynamic-update-slice_fusion
  33.1 1.5 collective-permute-start
  34.6 1.3 collective-permute-start.1
  35.9 0.0 copy-start.4
  35.9 0.0 copy-start.6
  36.0 0.0 copy-start.8
  36.0 0.0 collective-permute-done
  36.0 3.5 %collective-permute-done.1 = bf16[2,2,384]{2,1,0:T(2,128)(2,1)S(1)} collective-permute-done((bf16[2,2,384]{2,1,0:T(2,128)(2,1)S(1)}, bf16[2,2,384]{2,1,0:T(2,128)(2,1)S(1)}, u32[]{:S(2)}, u32[]{:S(2)}) %collective-permute-start.1) | collective-permute-done | bytes 3104 | tf_op jit(solution)/shard_map/ppermute | solution.py:67
  39.5 0.2 multiply_reduce_fusion
  39.7 0.3 multiply_convert_fusion
  40.1 0.5 convolution_convert_fusion
  40.6 0.4 fusion.14
  41.0 0.4 fusion.13
  41.5 0.4 fusion.12
  41.9 0.4 fusion.11
  42.3 0.4 fusion.10
  42.8 0.0 copy-start.1
  42.8 1.6 %copy-done.1 = f32[5,384,384]{2,1,0:T(8,128)} copy-done((f32[5,384,384]{2,1,0:T(8,128)}, f32[5,384,384]{2,1,0:T(8,128)S(1)}, u32[]{:S(2)}) %copy-start.1) | copy-done | bytes 2949144
  44.3 0.1 slice.356
  44.4 4.5 %collective-permute-start.3 = (bf16[5,192,384]{2,1,0:T(8,128)(2,1)S(1)}, bf16[5,192,384]{2,1,0:T(8,128)(2,1)}, u32[]{:S(2)}, u32[]{:S(2)}) collective-permute-start(bf16[5,192,384]{2,1,0:T(8,128)(2,1)S(1)} %slice.356), channel_id=1, source_target_pairs={{0,1},{1,0},{2,3},{3,2},{4,5},{5,4},{6,7},{7,6},{8,9},{9,8},{10,11... | collective-permute-start | bytes 2211848 | tf_op jit(solution)/shard_map/ppermute | solution.py:88
  49.0 6.4 %all-to-all-done = bf16[32,2,384]{2,1,0:T(2,128)(2,1)S(1)} async-done(((bf16[32,2,384]{2,1,0:T(2,128)(2,1)}), bf16[32,2,384]{2,1,0:T(2,128)(2,1)S(1)}, u32[]{:S(2)}, u32[]{:S(2)}) %all-to-all-start) | async-done | bytes 49184 | tf_op jit(solution)/shard_map/all_to_all | solution.py:57
  55.4 1.0 broadcast_in_dim.18
  56.4 7.5 %all-to-all-start.1 = ((bf16[16,64,384]{2,1,0:T(8,128)(2,1)}), bf16[16,64,384]{2,1,0:T(8,128)(2,1)S(1)}, u32[]{:S(2)}, u32[]{:S(2)}) async-start(bf16[16,64,384]{2,1,0:T(8,128)(2,1)} %broadcast_in_dim.18), calls=%async_computation.1 | async-start | bytes 1572864 | tf_op jit(solution)/shard_map/all_to_all | solution.py:59
  63.9 0.0 collective-permute-done.3
  63.9 1.7 %fusion = bf16[5,192,384]{2,1,0:T(8,128)(2,1)S(1)} fusion(f32[5,384,384]{2,1,0:T(8,128)} %copy-done.1, bf16[5,192,384]{2,1,0:T(8,128)(2,1)} %collective-permute-done.3), kind=kLoop, calls=%fused_computation.10 | loop fusion | flops 1105920 | bytes 2949120 | tf_op jit(solution)/shard_map/convert_element_type | solution.py:89
  65.6 1.0 pad.4
  66.7 7.2 %all-to-all-done.1 = bf16[16,64,384]{2,1,0:T(8,128)(2,1)S(1)} async-done(((bf16[16,64,384]{2,1,0:T(8,128)(2,1)}), bf16[16,64,384]{2,1,0:T(8,128)(2,1)S(1)}, u32[]{:S(2)}, u32[]{:S(2)}) %all-to-all-start.1) | async-done | bytes 786464 | tf_op jit(solution)/shard_map/all_to_all | solution.py:59
  73.9 6.4 %all-to-all-start.2 = ((bf16[16,64,384]{2,1,0:T(8,128)(2,1)}), bf16[16,64,384]{2,1,0:T(8,128)(2,1)}, u32[]{:S(2)}, u32[]{:S(2)}) async-start(bf16[16,64,384]{2,1,0:T(8,128)(2,1)} %pad.4), calls=%async_computation.2 | async-start | bytes 1572864 | tf_op jit(solution)/shard_map/all_to_all | solution.py:91
  80.3 0.1 slice.195
  80.3 1.9 %collective-permute-start.2 = (bf16[5,192,384]{2,1,0:T(8,128)(2,1)S(1)}, bf16[5,192,384]{2,1,0:T(8,128)(2,1)S(1)}, u32[]{:S(2)}, u32[]{:S(2)}) collective-permute-start(bf16[5,192,384]{2,1,0:T(8,128)(2,1)S(1)} %bitcast.72), channel_id=1, source_target_pairs={{0,1},{1,0},{2,3},{3,2},{4,5},{5,4},{6,7},{7,6},{8,9},{9,8},{10,11... | collective-permute-start | bytes 2211848 | tf_op jit(solution)/shard_map/ppermute | solution.py:62
  82.3 1.0 maximum_convert_fusion
  83.2 0.1 slice.169
  83.3 6.4 %all-to-all-done.2 = bf16[16,64,384]{2,1,0:T(8,128)(2,1)} async-done(((bf16[16,64,384]{2,1,0:T(8,128)(2,1)}), bf16[16,64,384]{2,1,0:T(8,128)(2,1)}, u32[]{:S(2)}, u32[]{:S(2)}) %all-to-all-start.2) | async-done | bytes 786464 | tf_op jit(solution)/shard_map/all_to_all | solution.py:91
  89.7 1.2 add_add_fusion
  90.9 0.1 reshape.131
  90.9 0.8 slice_convert_fusion.1
  91.7 0.1 reshape.120
  91.8 0.7 add_convert_fusion.1
  92.5 19.2 %all-to-all-start.3 = ((bf16[32,2,384]{2,1,0:T(2,128)(2,1)}), bf16[32,2,384]{2,1,0:T(2,128)(2,1)S(1)}, u32[]{:S(2)}, u32[]{:S(2)}) async-start(bf16[32,2,384]{2,1,0:T(2,128)(2,1)} %add_convert_fusion.1), calls=%async_computation.3 | async-start | bytes 98304 | tf_op jit(solution)/shard_map/all_to_all | solution.py:93
  111.7 0.0 collective-permute-done.2
  111.8 1.3 fusion.43
  113.1 1.3 fusion.52
  114.4 1.3 fusion.45
  115.7 1.3 fusion.80
  116.9 1.3 fusion.47
  118.2 1.3 fusion.55
  119.5 1.3 fusion.58
  120.8 1.3 fusion.61
  122.2 0.0 copy-done.7
  122.2 3.6 %fusion.15 = bf16[1,512,384]{2,1,0:T(8,128)(2,1)} fusion(f32[512,384]{1,0:T(8,128)} %fusion.52, f32[512,384]{1,0:T(8,128)} %fusion.55, f32[512,384]{1,0:T(8,128)} %fusion.58, f32[512,384]{1,0:T(8,128)} %fusion.61, f32[516,384]{1,0:T(8,128)} %maximum_convert_fusion, bf16[516,384]{1,0:T(8,128)(2,1)S(1)} %get-tuple-element.3, ...), kind=kOutput, calls=%fused_computation.38 | convolution fusion | flops 312508416 | bytes 6206980 | tf_op jit(solution)/shard_map/dot_general | solution.py:113
  125.8 3.5 %multiply_reduce_fusion.1 = (f32[512]{0:T(512)S(1)}, f32[512,384]{1,0:T(8,128)}) fusion(f32[516,384]{1,0:T(8,128)S(1)} %get-tuple-element.4, f32[512,384]{1,0:T(8,128)} %fusion.43, f32[512,384]{1,0:T(8,128)} %fusion.45, f32[512,384]{1,0:T(8,128)} %fusion.80, f32[512,384]{1,0:T(8,128)} %fusion.47, bf16[5,192,384]{2,1,0:T(8,128)(2,1)S(1)} %bitcast.81, ...), kind=kOutput, calls=%fused_computation.59 | convolution fusion | flops 154533376 | bytes 6588416 | tf_op jit(solution)/shard_map/dot_general | solution.py:110
  129.3 6.3 %all-to-all-done.3 = bf16[32,2,384]{2,1,0:T(2,128)(2,1)S(1)} async-done(((bf16[32,2,384]{2,1,0:T(2,128)(2,1)}), bf16[32,2,384]{2,1,0:T(2,128)(2,1)S(1)}, u32[]{:S(2)}, u32[]{:S(2)}) %all-to-all-start.3) | async-done | bytes 49184 | tf_op jit(solution)/shard_map/all_to_all | solution.py:93
  135.6 0.1 convert_reduce_fusion
  135.6 0.6 broadcast_in_dim.21
  136.3 5.8 %all-to-all-start.4 = ((f32[16,2,384]{2,1,0:T(2,128)}), f32[16,2,384]{2,1,0:T(2,128)S(1)}, u32[]{:S(2)}, u32[]{:S(2)}) async-start(f32[16,2,384]{2,1,0:T(2,128)} %broadcast_in_dim.21), calls=%async_computation.4 | async-start | bytes 98304 | tf_op jit(solution)/shard_map/all_to_all | solution.py:95
  142.1 2.2 %fusion.50 = bf16[1,512,384]{2,1,0:T(8,128)(2,1)} fusion(f32[512]{0:T(512)S(1)} %slice.169, f32[512,384]{1,0:T(8,128)} %get-tuple-element.12, f32[512]{0:T(512)S(1)} %broadcast_multiply_fusion.1, f32[516,384]{1,0:T(8,128)S(1)} %get-tuple-element.4, bf16[1,512,384]{2,1,0:T(8,128)(2,1)S(1)} %copy-done.3), kind=kLoop, calls=%fused_computation.92 | loop fusion | flops 1179648 | bytes 2363392 | tf_op jit(solution)/shard_map/broadcast_in_dim | solution.py:120
  144.3 4.1 %all-to-all-done.4 = f32[16,2,384]{2,1,0:T(2,128)S(1)} async-done(((f32[16,2,384]{2,1,0:T(2,128)}), f32[16,2,384]{2,1,0:T(2,128)S(1)}, u32[]{:S(2)}, u32[]{:S(2)}) %all-to-all-start.4) | async-done | bytes 49184 | tf_op jit(solution)/shard_map/all_to_all | solution.py:95
  148.4 0.7 reshape.108
  (27 shorter events, 0.2 us)
Async XLA Ops:
  0.6 38.9 %copy-start = (bf16[1,512,384]{2,1,0:T(8,128)(2,1)S(1)}, bf16[1,512,384]{2,1,0:T(8,128)(2,1)}, u32[]{:S(2)}) copy-start(bf16[1,512,384]{2,1,0:T(8,128)(2,1)} %param.3) | copy-start | bytes 1179652
  2.2 53.2 %all-to-all-start = ((bf16[32,2,384]{2,1,0:T(2,128)(2,1)}), bf16[32,2,384]{2,1,0:T(2,128)(2,1)S(1)}, u32[]{:S(2)}, u32[]{:S(2)}) async-start(bf16[32,2,384]{2,1,0:T(2,128)(2,1)} %broadcast_in_dim.17), calls=%async_computation | async-start | bytes 98304 | tf_op jit(solution)/shard_map/all_to_all | solution.py:57
  31.9 8.1 %copy-start.2 = (bf16[1,512,384]{2,1,0:T(8,128)(2,1)S(1)}, bf16[1,512,384]{2,1,0:T(8,128)(2,1)}, u32[]{:S(2)}) copy-start(bf16[1,512,384]{2,1,0:T(8,128)(2,1)} %param.5) | copy-start | bytes 1179652
  33.1 2.9 %collective-permute-start = (bf16[2,2,384]{2,1,0:T(2,128)(2,1)S(1)}, bf16[2,2,384]{2,1,0:T(2,128)(2,1)S(1)}, u32[]{:S(2)}, u32[]{:S(2)}) collective-permute-start(bf16[2,2,384]{2,1,0:T(2,128)(2,1)S(1)} %get-tuple-element.5), channel_id=1, source_target_pairs={{0,1},{1,2},{2,3},{3,4},{4,5},{5,6},{6,7},{7,8},{8,9},{9,10},{10,1... | collective-permute-start | bytes 9224 | tf_op jit(solution)/shard_map/ppermute | solution.py:66
  34.6 4.9 %collective-permute-start.1 = (bf16[2,2,384]{2,1,0:T(2,128)(2,1)S(1)}, bf16[2,2,384]{2,1,0:T(2,128)(2,1)S(1)}, u32[]{:S(2)}, u32[]{:S(2)}) collective-permute-start(bf16[2,2,384]{2,1,0:T(2,128)(2,1)S(1)} %get-tuple-element.6), channel_id=1, source_target_pairs={{1,0},{2,1},{3,2},{4,3},{5,4},{6,5},{7,6},{8,7},{9,8},{10,9},{11,1... | collective-permute-start | bytes 9224 | tf_op jit(solution)/shard_map/ppermute | solution.py:67
  35.9 4.7 %copy-start.4 = (pred[384]{0:T(512)(128)(4,1)}, pred[384]{0:T(512)(128)(4,1)S(1)}, u32[]{:S(2)}) copy-start(pred[384]{0:T(512)(128)(4,1)S(1)} %get-tuple-element.19) | copy-start | bytes 1156
  35.9 4.7 %copy-start.6 = (pred[384]{0:T(512)(128)(4,1)}, pred[384]{0:T(512)(128)(4,1)S(1)}, u32[]{:S(2)}) copy-start(pred[384]{0:T(512)(128)(4,1)S(1)} %get-tuple-element.20) | copy-start | bytes 1156
  36.0 4.7 %copy-start.8 = (pred[384]{0:T(512)(128)(4,1)}, pred[384]{0:T(512)(128)(4,1)S(1)}, u32[]{:S(2)}) copy-start(pred[384]{0:T(512)(128)(4,1)S(1)} %fusion.91) | copy-start | bytes 1156
  42.8 1.6 %copy-start.1 = (f32[5,384,384]{2,1,0:T(8,128)}, f32[5,384,384]{2,1,0:T(8,128)S(1)}, u32[]{:S(2)}) copy-start(f32[5,384,384]{2,1,0:T(8,128)S(1)} %fusion.10) | copy-start | bytes 8847364
  44.4 19.5 %collective-permute-start.3 = (bf16[5,192,384]{2,1,0:T(8,128)(2,1)S(1)}, bf16[5,192,384]{2,1,0:T(8,128)(2,1)}, u32[]{:S(2)}, u32[]{:S(2)}) collective-permute-start(bf16[5,192,384]{2,1,0:T(8,128)(2,1)S(1)} %slice.356), channel_id=1, source_target_pairs={{0,1},{1,0},{2,3},{3,2},{4,5},{5,4},{6,7},{7,6},{8,9},{9,8},{10,11... | collective-permute-start | bytes 2211848 | tf_op jit(solution)/shard_map/ppermute | solution.py:88
  56.4 17.5 %all-to-all-start.1 = ((bf16[16,64,384]{2,1,0:T(8,128)(2,1)}), bf16[16,64,384]{2,1,0:T(8,128)(2,1)S(1)}, u32[]{:S(2)}, u32[]{:S(2)}) async-start(bf16[16,64,384]{2,1,0:T(8,128)(2,1)} %broadcast_in_dim.18), calls=%async_computation.1 | async-start | bytes 1572864 | tf_op jit(solution)/shard_map/all_to_all | solution.py:59
  73.9 15.8 %all-to-all-start.2 = ((bf16[16,64,384]{2,1,0:T(8,128)(2,1)}), bf16[16,64,384]{2,1,0:T(8,128)(2,1)}, u32[]{:S(2)}, u32[]{:S(2)}) async-start(bf16[16,64,384]{2,1,0:T(8,128)(2,1)} %pad.4), calls=%async_computation.2 | async-start | bytes 1572864 | tf_op jit(solution)/shard_map/all_to_all | solution.py:91
  80.3 31.4 %collective-permute-start.2 = (bf16[5,192,384]{2,1,0:T(8,128)(2,1)S(1)}, bf16[5,192,384]{2,1,0:T(8,128)(2,1)S(1)}, u32[]{:S(2)}, u32[]{:S(2)}) collective-permute-start(bf16[5,192,384]{2,1,0:T(8,128)(2,1)S(1)} %bitcast.72), channel_id=1, source_target_pairs={{0,1},{1,0},{2,3},{3,2},{4,5},{5,4},{6,7},{7,6},{8,9},{9,8},{10,11... | collective-permute-start | bytes 2211848 | tf_op jit(solution)/shard_map/ppermute | solution.py:62
  92.5 43.1 %all-to-all-start.3 = ((bf16[32,2,384]{2,1,0:T(2,128)(2,1)}), bf16[32,2,384]{2,1,0:T(2,128)(2,1)S(1)}, u32[]{:S(2)}, u32[]{:S(2)}) async-start(bf16[32,2,384]{2,1,0:T(2,128)(2,1)} %add_convert_fusion.1), calls=%async_computation.3 | async-start | bytes 98304 | tf_op jit(solution)/shard_map/all_to_all | solution.py:93
  120.8 1.3 copy-start.5
  120.8 1.3 copy-start.7
  120.8 1.3 copy-start.9
  125.8 16.3 %copy-start.3 = (bf16[1,512,384]{2,1,0:T(8,128)(2,1)S(1)}, bf16[1,512,384]{2,1,0:T(8,128)(2,1)}, u32[]{:S(2)}) copy-start(bf16[1,512,384]{2,1,0:T(8,128)(2,1)} %param.5) | copy-start | bytes 1179652
  136.3 12.1 %all-to-all-start.4 = ((f32[16,2,384]{2,1,0:T(2,128)}), f32[16,2,384]{2,1,0:T(2,128)S(1)}, u32[]{:S(2)}, u32[]{:S(2)}) async-start(f32[16,2,384]{2,1,0:T(2,128)} %broadcast_in_dim.21), calls=%async_computation.4 | async-start | bytes 98304 | tf_op jit(solution)/shard_map/all_to_all | solution.py:95

commit v2 on v1

v2 whole, which is shorter than its diff:
```python
import functools

import jax
import jax.numpy as jnp
from jax import lax
from jax.experimental import pallas as pl
from jax.experimental.pallas import tpu as pltpu
from jax.sharding import Mesh, PartitionSpec as P

XY = ("x", "y")
SEQ = ("z", "core")
BF = jnp.bfloat16
F32 = jnp.float32
TOP = 8
VMEM_BYTES = 24 * 1024 * 1024


def call(body, out_shape, flops, bytes_accessed, scalars=0, plain=0, scratch=()):
    specs = [pl.BlockSpec(memory_space=pltpu.SMEM)] * scalars
    specs += [pl.BlockSpec(memory_space=pltpu.VMEM)] * plain
    outs = jax.tree.map(lambda _: pl.BlockSpec(memory_space=pltpu.VMEM), out_shape)
    return pl.pallas_call(
        body,
        out_shape=out_shape,
        in_specs=specs,
        out_specs=outs,
        scratch_shapes=list(scratch),
        compiler_params=pltpu.CompilerParams(vmem_limit_bytes=VMEM_BYTES),
        cost_estimate=pl.CostEstimate(
            flops=flops, bytes_accessed=bytes_accessed, transcendentals=0
        ),
    )


def norm(rows):
    inputs = rows.astype(F32)
    scale = jnp.sqrt(jnp.mean(inputs * inputs, axis=-1, keepdims=True) + 1e-05)
    return inputs, scale, inputs / scale


def cumulative(values):
    return 0.5 * (1.0 + lax.erf(values * 0.7071067811865476))


def gelu_rows(rows):
    normed = norm(rows)[2]
    return (normed * cumulative(normed)).astype(BF)


def order_rows(core, width, depth):
    half = width // 2
    held = width // (2 * depth)
    j = lax.broadcasted_iota(jnp.int32, (width, 1), 0)
    side = (j >= half).astype(jnp.int32)
    within = j - side * half
    pair = within // (2 * depth)
    member = (within // depth) % 2
    place = within % depth
    source = (place * 2 + (side + core) % 2) * held + 2 * pair + member
    o = lax.broadcasted_iota(jnp.int32, (width, width), 1)
    return jnp.where(o == source, 1.0, 0.0).astype(BF)


def turn(a, b):
    return lax.dot_general(a, b, (((1,), (1,)), ((), ())), preferred_element_type=F32)


def act_body(depth, core_ref, x_ref, g_ref, act_ref, cot_t_ref):
    order = order_rows(core_ref[0], x_ref.shape[1], depth)
    cot_t_ref[...] = turn(order, g_ref[...]).astype(BF)
    act_ref[...] = gelu_rows(x_ref[...])


def grad_body(taps, act_ref, cot_t_ref, before_ref, after_ref, mine_ref, other_ref, pad_ref):
    length, width = act_ref.shape
    edge = (taps - 1) // 2
    half = width // 2
    pad_ref[TOP - edge : TOP] = gelu_rows(before_ref[...]).astype(F32)
    pad_ref[TOP : TOP + length] = act_ref[...].astype(F32)
    pad_ref[TOP + length : TOP + length + edge] = gelu_rows(after_ref[...]).astype(F32)
    cot_t = cot_t_ref[...]
    for shift in range(taps):
        begin = TOP - edge + shift
        window = pad_ref[begin : begin + length].astype(BF)
        part = jnp.dot(cot_t, window, preferred_element_type=F32)
        mine_ref[shift] = part[:half]
        other_ref[shift] = part[half:].astype(BF)


def slope_body(depth, core_ref, x_ref, g_ref, before_ref, after_ref, slope_ref, pad_ref):
    length, width = x_ref.shape
    edge = before_ref.shape[0]
    order = order_rows(core_ref[0], width, depth)
    pad_ref[TOP - edge : TOP] = turn(before_ref[...], order)
    pad_ref[TOP : TOP + length] = turn(g_ref[...], order)
    pad_ref[TOP + length : TOP + length + edge] = turn(after_ref[...], order)
    normed = norm(x_ref[...])[2]
    slope_ref[...] = cumulative(normed) + normed * jnp.exp(-0.5 * normed * normed) * (
        0.3989422804014327
    )


def pair_body(mine_ref, got_ref, out_ref):
    blocks = mine_ref.shape[0]
    out_ref[:blocks] = (mine_ref[...] + got_ref[...].astype(F32)).astype(BF)
    for extra in range(blocks, out_ref.shape[0]):
        out_ref[extra] = jnp.zeros(out_ref.shape[1:], BF)


def plane_body(depth, plane_ref, row_ref, out_ref):
    total = plane_ref[0].astype(F32)
    for i in range(1, plane_ref.shape[0]):
        total = total + plane_ref[i].astype(F32)
    rows = row_ref[...].astype(F32)
    out_ref[0] = jnp.broadcast_to(rows[0:1], out_ref.shape[1:]).astype(BF)
    out_ref[1] = jnp.broadcast_to(rows[1:2], out_ref.shape[1:]).astype(BF)
    out_ref[2] = total[:depth].astype(BF)
    out_ref[3] = total[depth:].astype(BF)


def line_body(share, line_ref, out_ref):
    depth, width = line_ref.shape[1:]
    first = jnp.sum(line_ref[2].astype(F32), axis=0, keepdims=True) / share
    second = jnp.sum(line_ref[3].astype(F32), axis=0, keepdims=True) / share
    both = jnp.concatenate([first, second], axis=0)
    high = both.astype(BF).astype(F32)
    tail = jnp.concatenate([high, both - high, jnp.zeros((4, width), F32)], axis=0).astype(BF)
    for i in range(out_ref.shape[0]):
        out_ref[i, :depth] = line_ref[0]
        out_ref[i, depth : 2 * depth] = line_ref[1]
        out_ref[i, 2 * depth :] = tail


def conv_body(
    taps,
    depth,
    core_ref,
    x_ref,
    g_ref,
    slope_ref,
    act_pad_ref,
    cot_pad_ref,
    own_ref,
    far_ref,
    out_ref,
    grad_ref,
):
    length, width = x_ref.shape
    edge = (taps - 1) // 2
    pairs = width // (4 * depth)
    order = order_rows(core_ref[0], width, depth)
    weights = [
        jnp.concatenate(
            [
                ref[shift * pairs + i, : 2 * depth]
                for ref in (own_ref, far_ref)
                for i in range(pairs)
            ],
            axis=0,
        )
        for shift in range(taps)
    ]
    rows = length // 2
    for begin in range(0, length, rows):
        at = TOP - edge + begin
        total = jnp.zeros((rows, width), F32)
        carry = jnp.zeros((rows, width), F32)
        for shift in range(taps):
            window = act_pad_ref[at + shift : at + shift + rows].astype(BF)
            total = total + turn(window, weights[shift])
            back = at + 2 * edge - shift
            window = cot_pad_ref[back : back + rows].astype(BF)
            carry = carry + jnp.dot(window, weights[shift], preferred_element_type=F32)
        branch = jnp.dot(total.astype(BF), order, preferred_element_type=F32)
        inputs, scale, normed = norm(x_ref[begin : begin + rows])
        out_ref[begin : begin + rows] = (inputs + branch).astype(BF)
        normed_grad = carry * slope_ref[begin : begin + rows]
        project = jnp.mean(normed_grad * normed, axis=-1, keepdims=True)
        grad_ref[begin : begin + rows] = (
            g_ref[begin : begin + rows].astype(F32) + (normed_grad - normed * project) / scale
        ).astype(BF)


def local(section_input, kernel, cotangent):
    x = section_input[0]
    g = cotangent[0]
    length, width = x.shape
    held, taps, _ = kernel.shape
    edge = (taps - 1) // 2
    depth = lax.axis_size("z")
    groups = lax.axis_size(XY)
    count = lax.axis_size(SEQ)
    pairs = held // 2
    blocks = taps * pairs
    half = width // 2
    padded = length + 2 * TOP
    core = lax.axis_index("core").astype(jnp.int32).reshape(1)
    spot = lax.axis_index(XY)
    shape = jax.ShapeDtypeStruct
    swap = [(0, 1), (1, 0)]
    macs = length * width * width

    ends = jnp.concatenate([x[length - edge :], g[length - edge :]], axis=0)
    starts = jnp.concatenate([x[:edge], g[:edge]], axis=0)
    before = lax.ppermute(ends, SEQ, [(i, i + 1) for i in range(count - 1)])
    after = lax.ppermute(starts, SEQ, [(i + 1, i) for i in range(count - 1)])

    act, cot_t = call(
        functools.partial(act_body, depth),
        (shape((length, width), BF), shape((width, length), BF)),
        2 * macs,
        4 * length * width * 2,
        1,
        2,
    )(core, x, g)
    mine, other, act_pad = call(
        functools.partial(grad_body, taps),
        (
            shape((taps, half, width), F32),
            shape((taps, half, width), BF),
            shape((padded, width), F32),
        ),
        2 * taps * macs,
        8 * length * width * 2,
        0,
        4,
    )(act, cot_t, before[:edge], after[:edge])
    got = lax.ppermute(other, "core", swap)
    slope, cot_pad = call(
        functools.partial(slope_body, depth),
        (shape((length, width), F32), shape((padded, width), F32)),
        2 * macs,
        6 * length * width * 2,
        1,
        4,
    )(core, x, g, before[edge:], after[edge:])

    chip = call(
        pair_body,
        shape((groups, 2 * depth, width), BF),
        taps * half * width,
        taps * half * width * 8,
        0,
        2,
    )(mine.reshape(blocks, 2 * depth, width), got.reshape(blocks, 2 * depth, width))
    plane = lax.all_to_all(chip, XY, 0, 0)

    by_block = kernel.reshape(pairs, 2, taps, width).transpose(2, 0, 1, 3).reshape(blocks, 2, width)
    rows = lax.dynamic_index_in_dim(by_block, jnp.minimum(spot, blocks - 1), 0, keepdims=False)
    packed = call(
        functools.partial(plane_body, depth),
        shape((4, depth, width), BF),
        groups * 2 * depth * width,
        groups * 2 * depth * width * 2,
        0,
        2,
    )(plane, rows)
    line = lax.all_to_all(packed.transpose(1, 0, 2), "z", 0, 0).transpose(1, 0, 2)
    sent = call(
        functools.partial(line_body, float(groups * section_input.shape[0])),
        shape((groups, 2 * depth + 8, width), BF),
        4 * depth * width,
        groups * 2 * depth * width * 2,
        0,
        1,
    )(line)
    own = lax.all_to_all(sent, XY, 0, 0)
    far = lax.ppermute(own, "core", swap)

    sums = own[:blocks, 2 * depth : 2 * depth + 4].astype(F32)
    sums = (sums[:, :2] + sums[:, 2:]).reshape(taps, held, width)
    kernel_grad = sums.transpose(1, 0, 2)

    out, grad = call(
        functools.partial(conv_body, taps, depth),
        (shape((length, width), BF), shape((length, width), BF)),
        4 * taps * macs,
        12 * length * width * 2,
        1,
        7,
    )(core, x, g, slope, act_pad, cot_pad, own, far)
    return (out[None], grad[None], kernel_grad)


def solution(mesh):
    seq = mesh.shape["seq"]
    side = int(round(mesh.shape["dp"] ** 0.5))
    fine = Mesh(mesh.devices.reshape(side, side, seq // 2, 2), XY + SEQ)
    return jax.shard_map(
        local,
        mesh=fine,
        in_specs=(P(XY, SEQ, None), P(SEQ, None, None), P(XY, SEQ, None)),
        out_specs=(P(XY, SEQ, None), P(XY, SEQ, None), P(SEQ, None, None)),
        check_vma=False,
    )
```

time: 150 us -> 124 us (0.83)
  the two profiles are of different devices: /device:TPU:2 before, /device:TPU:1 now
where the time goes in v2:
time: 124 us; the launch traced here: 123 us
  blocking collectives  60.6 us (49%)
  starting transfers between devices  31.4 us (25%)
  waiting for transfers between devices  14.5 us (12%)
  Pallas kernels  7.95 us (6%)
  local copies, waits for them, and re-layouts  7.62 us (6%)
    all_to_all x1, blocking collectives, local(): lax.all_to_all(packed.transpose(1, 0, 2), 'z', 0, 0).transpose(1, 0, 2)  44.8 us
    ppermute x1, starting transfers between devices, local(): after = lax.ppermute(starts, SEQ, [(i + 1, i) for i in range(count - 1)])  16.1 us
    all_to_all x1, blocking collectives, local(): own = lax.all_to_all(sent, XY, 0, 0)  15.8 us
    all_to_all x1, waiting for transfers between devices, local(): plane = lax.all_to_all(chip, XY, 0, 0)  12.7 us
    ppermute x1, starting transfers between devices, local(): far = lax.ppermute(own, 'core', swap)  7.29 us
    unnamed x18, local copies, waits for them, and re-layouts  6.08 us
    pallas_call x1, Pallas kernels, local(): call(functools.partial(conv_body, taps, depth), (shape((length, width), B...  4.02 us
    all_to_all x1, starting transfers between devices, local(): plane = lax.all_to_all(chip, XY, 0, 0)  3.74 us
  transfers between devices with their start and end apart: 5, of which 2 were waited for; matrix products, arithmetic and copies ran while one was open for 1% of the time, Pallas kernels for 1%

profile of v2, /device:TPU:1, one launch (start us, length us, event | category | flops | bytes accessed | tf_op | source)
XLA Modules:
  0.0 123.0 jit_solution(14474706854661199136)
XLA Ops:
  0.6 0.8 slice_bitcast_fusion
  1.4 16.1 %collective-permute-start.1 = (bf16[4,384]{1,0:T(4,128)(2,1)S(1)}, bf16[4,384]{1,0:T(4,128)(2,1)S(1)}, u32[]{:S(2)}, u32[]{:S(2)}) collective-permute-start(bf16[4,384]{1,0:T(4,128)(2,1)S(1)} %pad_maximum_fusion.1), channel_id=1, source_target_pairs={{1,0},{2,1},{3,2},{4,3},{5,4},{6,5},{7,6},{8,7},{9,8},{10,9},{11,1... | collective-permute-start | bytes 9224 | tf_op jit(solution)/shard_map/ppermute | solution.py:206
  17.5 1.9 %collective-permute-start = (bf16[4,384]{1,0:T(4,128)(2,1)S(1)}, bf16[4,384]{1,0:T(4,128)(2,1)S(1)}, u32[]{:S(2)}, u32[]{:S(2)}) collective-permute-start(bf16[4,384]{1,0:T(4,128)(2,1)S(1)} %pad_maximum_fusion), channel_id=1, source_target_pairs={{0,1},{1,2},{2,3},{3,4},{4,5},{5,6},{6,7},{7,8},{8,9},{9,10},{10,1... | collective-permute-start | bytes 9224 | tf_op jit(solution)/shard_map/ppermute | solution.py:205
  19.4 0.0 copy-start
  19.4 1.0 copy-done
  20.4 0.0 copy-start.2
  20.4 1.0 copy-done.2
  21.4 0.5 shard_map.59
  22.0 0.0 collective-permute-done.1
  22.0 0.0 collective-permute-done
  22.0 1.3 %shard_map.60 = (f32[5,192,384]{2,1,0:T(8,128)S(1)}, bf16[5,192,384]{2,1,0:T(8,128)(2,1)S(1)}, f32[528,384]{1,0:T(8,128)S(1)}) custom-call(bf16[512,384]{1,0:T(8,128)(2,1)S(1)} %get-tuple-element.13.act_ref, bf16[384,512]{1,0:T(8,128)(2,1)S(1)} %get-tuple-element.14.cot_t_ref, bf16[2,384]{1,0:T(2,128)(2,1)S(1)} %get-tuple-element.27.before_ref, ...), custom_call_target="tpu_custom_call" | custom-call | flops 754974720 | bytes 3145728 | tf_op jit(solution)/shard_map/pallas_call | solution.py:216
  23.3 0.0 copy-start.6
  23.3 0.9 copy-done.6
  24.2 2.4 %collective-permute-start.2 = (bf16[5,192,384]{2,1,0:T(8,128)(2,1)S(1)}, bf16[5,192,384]{2,1,0:T(8,128)(2,1)S(1)}, u32[]{:S(2)}, u32[]{:S(2)}) collective-permute-start(bf16[5,192,384]{2,1,0:T(8,128)(2,1)S(1)} %get-tuple-element.18), channel_id=1, source_target_pairs={{0,1},{1,0},{2,3},{3,2},{4,5},{5,4},{6,7},{7,6},{8,9},{9,8},{10,11... | collective-permute-start | bytes 2211848 | tf_op jit(solution)/shard_map/ppermute | solution.py:228
  26.6 1.8 %collective-permute-done.2 = bf16[5,192,384]{2,1,0:T(8,128)(2,1)S(1)} collective-permute-done((bf16[5,192,384]{2,1,0:T(8,128)(2,1)S(1)}, bf16[5,192,384]{2,1,0:T(8,128)(2,1)S(1)}, u32[]{:S(2)}, u32[]{:S(2)}) %collective-permute-start.2) | collective-permute-done | bytes 737312 | tf_op jit(solution)/shard_map/ppermute | solution.py:228
  28.4 1.1 shard_map.61
  29.5 0.0 copy-start.8
  29.5 3.7 %all-to-all-start = ((bf16[16,64,384]{2,1,0:T(8,128)(2,1)}), bf16[16,64,384]{2,1,0:T(8,128)(2,1)S(1)}, u32[]{:S(2)}, u32[]{:S(2)}) async-start(bf16[16,64,384]{2,1,0:T(8,128)(2,1)} %shard_map.61), calls=%async_computation | async-start | bytes 1572864 | tf_op jit(solution)/shard_map/all_to_all | solution.py:246
  33.3 0.0 copy-done.8
  33.3 12.7 %all-to-all-done.plane_ref = bf16[16,64,384]{2,1,0:T(8,128)(2,1)S(1)} async-done(((bf16[16,64,384]{2,1,0:T(8,128)(2,1)}), bf16[16,64,384]{2,1,0:T(8,128)(2,1)S(1)}, u32[]{:S(2)}, u32[]{:S(2)}) %all-to-all-start) | async-done | bytes 786464 | tf_op jit(solution)/shard_map/all_to_all | solution.py:246
  46.0 0.1 shard_map.62
  46.1 0.1 copy.6
  46.2 44.8 %all_to_all.15 = bf16[32,4,384]{2,1,0:T(4,128)(2,1)S(1)} all-to-all(bf16[32,4,384]{2,1,0:T(4,128)(2,1)S(1)} %copy.6), channel_id=1, replica_groups=mesh['x'=4,'y'=4,'z'=32,'core'=2] {'z'}, dimensions={0} | all-to-all | bytes 196608 | tf_op jit(solution)/shard_map/all_to_all | solution.py:258
  91.0 0.0 copy-start.1
  91.0 0.0 copy-start.3
  91.0 0.1 shard_map.63
  91.1 15.8 %all_to_all.16.own_ref = bf16[16,72,384]{2,1,0:T(8,128)(2,1)S(1)} all-to-all(bf16[16,72,384]{2,1,0:T(8,128)(2,1)S(1)} %shard_map.63), channel_id=1, replica_groups=mesh['x'=4,'y'=4,'z'=32,'core'=2] {'x','y'}, dimensions={0} | all-to-all | bytes 1769472 | tf_op jit(solution)/shard_map/all_to_all | solution.py:267
  106.9 7.3 %collective-permute-start.3 = (bf16[16,72,384]{2,1,0:T(8,128)(2,1)S(1)}, bf16[16,72,384]{2,1,0:T(8,128)(2,1)S(1)}, u32[]{:S(2)}, u32[]{:S(2)}) collective-permute-start(bf16[16,72,384]{2,1,0:T(8,128)(2,1)S(1)} %all_to_all.16.own_ref), channel_id=1, source_target_pairs={{0,1},{1,0},{2,3},{3,2},{4,5},{5,4},{6,7},{7,6},{8,9},{9,8},{10,11... | collective-permute-start | bytes 2654216 | tf_op jit(solution)/shard_map/ppermute | solution.py:268
  114.2 0.0 copy-done.1
  114.2 0.0 copy-done.3
  114.2 0.8 shard_map.58
  115.1 0.0 copy-start.4
  115.1 0.9 copy-done.4
  116.1 0.7 reshape.33
  116.7 0.0 collective-permute-done.3.far_ref
  116.7 0.0 copy-start.5
  116.7 1.1 copy-done.5
  117.9 0.0 copy-start.7
  117.9 1.1 copy-done.7
  119.0 4.0 %shard_map.64 = (bf16[512,384]{1,0:T(8,128)(2,1)}, bf16[512,384]{1,0:T(8,128)(2,1)}) custom-call(s32[1]{0:T(128)} %bitcast.core_ref, bf16[512,384]{1,0:T(8,128)(2,1)S(1)} %bitcast.29, bf16[512,384]{1,0:T(8,128)(2,1)S(1)} %bitcast.32, f32[512,384]{1,0:T(8,128)S(1)} %copy-done.5, f32[528,384]{1,0:T(8,128)S(1)} %copy-done.7, ...), custom_call_target="tpu_custom_call" | custom-call | flops 1509949440 | bytes 4718592 | tf_op jit(solution)/shard_map/pallas_call | solution.py:274
  (9 shorter events, 0.1 us)
Async XLA Ops:
  1.4 20.6 %collective-permute-start.1 = (bf16[4,384]{1,0:T(4,128)(2,1)S(1)}, bf16[4,384]{1,0:T(4,128)(2,1)S(1)}, u32[]{:S(2)}, u32[]{:S(2)}) collective-permute-start(bf16[4,384]{1,0:T(4,128)(2,1)S(1)} %pad_maximum_fusion.1), channel_id=1, source_target_pairs={{1,0},{2,1},{3,2},{4,3},{5,4},{6,5},{7,6},{8,7},{9,8},{10,9},{11,1... | collective-permute-start | bytes 9224 | tf_op jit(solution)/shard_map/ppermute | solution.py:206
  17.5 4.5 %collective-permute-start = (bf16[4,384]{1,0:T(4,128)(2,1)S(1)}, bf16[4,384]{1,0:T(4,128)(2,1)S(1)}, u32[]{:S(2)}, u32[]{:S(2)}) collective-permute-start(bf16[4,384]{1,0:T(4,128)(2,1)S(1)} %pad_maximum_fusion), channel_id=1, source_target_pairs={{0,1},{1,2},{2,3},{3,4},{4,5},{5,6},{6,7},{7,8},{8,9},{9,10},{10,1... | collective-permute-start | bytes 9224 | tf_op jit(solution)/shard_map/ppermute | solution.py:205
  19.4 1.0 copy-start
  20.4 1.0 copy-start.2
  23.3 0.9 copy-start.6
  24.2 4.2 %collective-permute-start.2 = (bf16[5,192,384]{2,1,0:T(8,128)(2,1)S(1)}, bf16[5,192,384]{2,1,0:T(8,128)(2,1)S(1)}, u32[]{:S(2)}, u32[]{:S(2)}) collective-permute-start(bf16[5,192,384]{2,1,0:T(8,128)(2,1)S(1)} %get-tuple-element.18), channel_id=1, source_target_pairs={{0,1},{1,0},{2,3},{3,2},{4,5},{5,4},{6,7},{7,6},{8,9},{9,8},{10,11... | collective-permute-start | bytes 2211848 | tf_op jit(solution)/shard_map/ppermute | solution.py:228
  29.5 3.8 %copy-start.8 = (bf16[6,5,384]{2,0,1:T(8,128)(2,1)S(1)}, bf16[6,5,384]{2,0,1:T(8,128)(2,1)}, u32[]{:S(2)}) copy-start(bf16[6,5,384]{2,0,1:T(8,128)(2,1)} %param.4) | copy-start | bytes 69124
  29.5 16.5 %all-to-all-start = ((bf16[16,64,384]{2,1,0:T(8,128)(2,1)}), bf16[16,64,384]{2,1,0:T(8,128)(2,1)S(1)}, u32[]{:S(2)}, u32[]{:S(2)}) async-start(bf16[16,64,384]{2,1,0:T(8,128)(2,1)} %shard_map.61), calls=%async_computation | async-start | bytes 1572864 | tf_op jit(solution)/shard_map/all_to_all | solution.py:246
  91.0 23.3 %copy-start.1 = (bf16[1,512,384]{2,1,0:T(8,128)(2,1)S(1)}, bf16[1,512,384]{2,1,0:T(8,128)(2,1)}, u32[]{:S(2)}) copy-start(bf16[1,512,384]{2,1,0:T(8,128)(2,1)} %param.3) | copy-start | bytes 1179652
  91.0 23.3 %copy-start.3 = (bf16[1,512,384]{2,1,0:T(8,128)(2,1)S(1)}, bf16[1,512,384]{2,1,0:T(8,128)(2,1)}, u32[]{:S(2)}) copy-start(bf16[1,512,384]{2,1,0:T(8,128)(2,1)} %param.5) | copy-start | bytes 1179652
  106.9 9.8 %collective-permute-start.3 = (bf16[16,72,384]{2,1,0:T(8,128)(2,1)S(1)}, bf16[16,72,384]{2,1,0:T(8,128)(2,1)S(1)}, u32[]{:S(2)}, u32[]{:S(2)}) collective-permute-start(bf16[16,72,384]{2,1,0:T(8,128)(2,1)S(1)} %all_to_all.16.own_ref), channel_id=1, source_target_pairs={{0,1},{1,0},{2,3},{3,2},{4,5},{5,4},{6,7},{7,6},{8,9},{9,8},{10,11... | collective-permute-start | bytes 2654216 | tf_op jit(solution)/shard_map/ppermute | solution.py:268
  115.1 0.9 copy-start.4
  116.7 1.1 copy-start.5
  117.9 1.1 copy-start.7

commit v3 on v2

--- a/solution.py
+++ b/solution.py
@@ -13,11 +13,13 @@
 F32 = jnp.float32
 TOP = 8
 VMEM_BYTES = 24 * 1024 * 1024
-
-
-def call(body, out_shape, flops, bytes_accessed, scalars=0, plain=0, scratch=()):
+ALONE_BYTES = 63 * 1024 * 1024
+
+
+def call(body, out_shape, flops, bytes_accessed, scalars=0, plain=0, scratch=(), far=0, vmem=VMEM_BYTES):
     specs = [pl.BlockSpec(memory_space=pltpu.SMEM)] * scalars
     specs += [pl.BlockSpec(memory_space=pltpu.VMEM)] * plain
+    specs += [pl.BlockSpec(memory_space=pltpu.HBM)] * far
     outs = jax.tree.map(lambda _: pl.BlockSpec(memory_space=pltpu.VMEM), out_shape)
     return pl.pallas_call(
         body,
@@ -25,7 +27,7 @@
         in_specs=specs,
         out_specs=outs,
         scratch_shapes=list(scratch),
-        compiler_params=pltpu.CompilerParams(vmem_limit_bytes=VMEM_BYTES),
+        compiler_params=pltpu.CompilerParams(vmem_limit_bytes=vmem),
         cost_estimate=pl.CostEstimate(
             flops=flops, bytes_accessed=bytes_accessed, transcendentals=0
         ),
@@ -65,39 +67,38 @@
     return lax.dot_general(a, b, (((1,), (1,)), ((), ())), preferred_element_type=F32)
 
 
-def act_body(depth, core_ref, x_ref, g_ref, act_ref, cot_t_ref):
+def act_body(depth, core_ref, x_hbm, g_hbm, act_ref, cot_t_ref, x_ref, g_ref, sems):
+    get_g = pltpu.make_async_copy(g_hbm, g_ref, sems.at[0])
+    get_x = pltpu.make_async_copy(x_hbm, x_ref, sems.at[1])
+    get_g.start()
+    get_x.start()
     order = order_rows(core_ref[0], x_ref.shape[1], depth)
+    get_g.wait()
     cot_t_ref[...] = turn(order, g_ref[...]).astype(BF)
+    get_x.wait()
     act_ref[...] = gelu_rows(x_ref[...])
 
 
-def grad_body(taps, act_ref, cot_t_ref, before_ref, after_ref, mine_ref, other_ref, pad_ref):
+def fill_act(pad_ref, act, before_ref, after_ref, edge):
+    length = act.shape[0]
+    pad_ref[TOP - edge : TOP] = gelu_rows(before_ref[:edge]).astype(F32)
+    pad_ref[TOP : TOP + length] = act.astype(F32)
+    pad_ref[TOP + length : TOP + length + edge] = gelu_rows(after_ref[:edge]).astype(F32)
+
+
+def grad_body(taps, pairs, act_ref, cot_t_ref, before_ref, after_ref, out_ref, pad_ref, *, side):
     length, width = act_ref.shape
     edge = (taps - 1) // 2
     half = width // 2
-    pad_ref[TOP - edge : TOP] = gelu_rows(before_ref[...]).astype(F32)
-    pad_ref[TOP : TOP + length] = act_ref[...].astype(F32)
-    pad_ref[TOP + length : TOP + length + edge] = gelu_rows(after_ref[...]).astype(F32)
-    cot_t = cot_t_ref[...]
+    rows = half // pairs
+    fill_act(pad_ref, act_ref[...], before_ref, after_ref, edge)
+    cot_t = cot_t_ref[side * half : (side + 1) * half]
     for shift in range(taps):
         begin = TOP - edge + shift
         window = pad_ref[begin : begin + length].astype(BF)
-        part = jnp.dot(cot_t, window, preferred_element_type=F32)
-        mine_ref[shift] = part[:half]
-        other_ref[shift] = part[half:].astype(BF)
-
-
-def slope_body(depth, core_ref, x_ref, g_ref, before_ref, after_ref, slope_ref, pad_ref):
-    length, width = x_ref.shape
-    edge = before_ref.shape[0]
-    order = order_rows(core_ref[0], width, depth)
-    pad_ref[TOP - edge : TOP] = turn(before_ref[...], order)
-    pad_ref[TOP : TOP + length] = turn(g_ref[...], order)
-    pad_ref[TOP + length : TOP + length + edge] = turn(after_ref[...], order)
-    normed = norm(x_ref[...])[2]
-    slope_ref[...] = cumulative(normed) + normed * jnp.exp(-0.5 * normed * normed) * (
-        0.3989422804014327
-    )
+        part = jnp.dot(cot_t, window, preferred_element_type=F32).astype(out_ref.dtype)
+        for i in range(pairs):
+            out_ref[shift * pairs + i] = part[i * rows : (i + 1) * rows]
 
 
 def pair_body(mine_ref, got_ref, out_ref):
@@ -131,50 +132,93 @@
         out_ref[i, 2 * depth :] = tail
 
 
-def conv_body(
+def weight(ref, shift, pairs, rows):
+    return jnp.concatenate([ref[shift * pairs + i, :rows] for i in range(pairs)], axis=0)
+
+
+def near_body(
     taps,
     depth,
     core_ref,
     x_ref,
     g_ref,
-    slope_ref,
-    act_pad_ref,
-    cot_pad_ref,
+    before_ref,
+    after_ref,
     own_ref,
-    far_ref,
-    out_ref,
-    grad_ref,
+    near_ref,
+    act_ref,
+    cot_ref,
+    kernel_grad_ref,
+    pad_ref,
 ):
     length, width = x_ref.shape
     edge = (taps - 1) // 2
     pairs = width // (4 * depth)
     order = order_rows(core_ref[0], width, depth)
-    weights = [
-        jnp.concatenate(
-            [
-                ref[shift * pairs + i, : 2 * depth]
-                for ref in (own_ref, far_ref)
-                for i in range(pairs)
-            ],
-            axis=0,
-        )
-        for shift in range(taps)
-    ]
+    fill_act(pad_ref, gelu_rows(x_ref[...]), before_ref, after_ref, edge)
+    act_ref[...] = pad_ref[...].astype(BF)
+    total = jnp.zeros((length, width // 2), F32)
+    for shift in range(taps):
+        begin = TOP - edge + shift
+        window = pad_ref[begin : begin + length].astype(BF)
+        total = total + turn(window, weight(own_ref, shift, pairs, 2 * depth))
+    near_ref[...] = total.astype(BF)
+    cot_ref[TOP : TOP + length] = turn(g_ref[...], order).astype(BF)
+    zeros = jnp.zeros((TOP - edge, width), F32)
+    first = turn(before_ref[edge:], order)
+    last = turn(after_ref[edge:], order)
+    cot_ref[:TOP] = jnp.concatenate([zeros, first], axis=0).astype(BF)
+    cot_ref[TOP + length :] = jnp.concatenate([last, zeros], axis=0).astype(BF)
+    for shift in range(taps):
+        for i in range(pairs):
+            value = own_ref[shift * pairs + i, 2 * depth :].astype(F32)
+            kernel_grad_ref[shift, 2 * i : 2 * i + 2] = value[:2] + value[2:4]
+
+
+def far_body(
+    taps,
+    depth,
+    core_ref,
+    x_ref,
+    g_ref,
+    near_ref,
+    act_ref,
+    cot_ref,
+    own_ref,
+    far_ref,
+    out_ref,
+    grad_ref,
+    act_pad_ref,
+    cot_pad_ref,
+):
+    length, width = x_ref.shape
+    edge = (taps - 1) // 2
+    pairs = width // (4 * depth)
+    act_pad_ref[...] = act_ref[...].astype(F32)
+    cot_pad_ref[...] = cot_ref[...].astype(F32)
+    order = order_rows(core_ref[0], width, depth)
+    own = [weight(own_ref, shift, pairs, 2 * depth) for shift in range(taps)]
+    far = [weight(far_ref, shift, pairs, 2 * depth) for shift in range(taps)]
     rows = length // 2
     for begin in range(0, length, rows):
         at = TOP - edge + begin
-        total = jnp.zeros((rows, width), F32)
+        total = jnp.zeros((rows, width // 2), F32)
         carry = jnp.zeros((rows, width), F32)
         for shift in range(taps):
-            window = act_pad_ref[at + shift : at + shift + rows].astype(BF)
-            total = total + turn(window, weights[shift])
             back = at + 2 * edge - shift
             window = cot_pad_ref[back : back + rows].astype(BF)
-            carry = carry + jnp.dot(window, weights[shift], preferred_element_type=F32)
-        branch = jnp.dot(total.astype(BF), order, preferred_element_type=F32)
+            both = jnp.concatenate([own[shift], far[shift]], axis=0)
+            carry = carry + jnp.dot(window, both, preferred_element_type=F32)
+            window = act_pad_ref[at + shift : at + shift + rows].astype(BF)
+            total = total + turn(window, far[shift])
+        grouped = jnp.concatenate([near_ref[begin : begin + rows], total.astype(BF)], axis=1)
+        branch = jnp.dot(grouped, order, preferred_element_type=F32)
         inputs, scale, normed = norm(x_ref[begin : begin + rows])
         out_ref[begin : begin + rows] = (inputs + branch).astype(BF)
-        normed_grad = carry * slope_ref[begin : begin + rows]
+        slope = cumulative(normed) + normed * jnp.exp(-0.5 * normed * normed) * (
+            0.3989422804014327
+        )
+        normed_grad = carry * slope
         project = jnp.mean(normed_grad * normed, axis=-1, keepdims=True)
         grad_ref[begin : begin + rows] = (
             g_ref[begin : begin + rows].astype(F32) + (normed_grad - normed * project) / scale
@@ -205,36 +249,34 @@
     before = lax.ppermute(ends, SEQ, [(i, i + 1) for i in range(count - 1)])
     after = lax.ppermute(starts, SEQ, [(i + 1, i) for i in range(count - 1)])
 
+    whole = pltpu.VMEM((length, width), BF)
+    pad = pltpu.VMEM((padded, width), F32)
     act, cot_t = call(
         functools.partial(act_body, depth),
         (shape((length, width), BF), shape((width, length), BF)),
         2 * macs,
         4 * length * width * 2,
         1,
+        0,
+        [whole, whole, pltpu.SemaphoreType.DMA((2,))],
         2,
+        ALONE_BYTES,
     )(core, x, g)
-    mine, other, act_pad = call(
-        functools.partial(grad_body, taps),
-        (
-            shape((taps, half, width), F32),
-            shape((taps, half, width), BF),
-            shape((padded, width), F32),
-        ),
-        2 * taps * macs,
-        8 * length * width * 2,
-        0,
-        4,
-    )(act, cot_t, before[:edge], after[:edge])
+    sides = [
+        call(
+            functools.partial(grad_body, taps, pairs, side=side),
+            shape((blocks, 2 * depth, width), kind),
+            taps * macs,
+            8 * length * width * 2,
+            0,
+            4,
+            [pad],
+        )
+        for side, kind in ((0, F32), (1, BF))
+    ]
+    other = sides[1](act, cot_t, before, after)
     got = lax.ppermute(other, "core", swap)
-    slope, cot_pad = call(
-        functools.partial(slope_body, depth),
-        (shape((length, width), F32), shape((padded, width), F32)),
-        2 * macs,
-        6 * length * width * 2,
-        1,
-        4,
-    )(core, x, g, before[edge:], after[edge:])
-
+    mine = sides[0](act, cot_t, before, after)
     chip = call(
         pair_body,
         shape((groups, 2 * depth, width), BF),
@@ -242,7 +284,7 @@
         taps * half * width * 8,
         0,
         2,
-    )(mine.reshape(blocks, 2 * depth, width), got.reshape(blocks, 2 * depth, width))
+    )(mine, got)
     plane = lax.all_to_all(chip, XY, 0, 0)
 
     by_block = kernel.reshape(pairs, 2, taps, width).transpose(2, 0, 1, 3).reshape(blocks, 2, width)
@@ -267,19 +309,30 @@
     own = lax.all_to_all(sent, XY, 0, 0)
     far = lax.ppermute(own, "core", swap)
 
-    sums = own[:blocks, 2 * depth : 2 * depth + 4].astype(F32)
-    sums = (sums[:, :2] + sums[:, 2:]).reshape(taps, held, width)
-    kernel_grad = sums.transpose(1, 0, 2)
-
+    near, act_rows, cot_rows, kernel_grad = call(
+        functools.partial(near_body, taps, depth),
+        (
+            shape((length, half), BF),
+            shape((padded, width), BF),
+            shape((padded, width), BF),
+            shape((taps, held, width), F32),
+        ),
+        2 * taps * macs,
+        8 * length * width * 2,
+        1,
+        5,
+        [pad],
+    )(core, x, g, before, after, own)
     out, grad = call(
-        functools.partial(conv_body, taps, depth),
+        functools.partial(far_body, taps, depth),
         (shape((length, width), BF), shape((length, width), BF)),
         4 * taps * macs,
         12 * length * width * 2,
         1,
         7,
-    )(core, x, g, slope, act_pad, cot_pad, own, far)
-    return (out[None], grad[None], kernel_grad)
+        [pad, pad],
+    )(core, x, g, near, act_rows, cot_rows, own, far)
+    return (out[None], grad[None], kernel_grad.transpose(1, 0, 2))
 
 
 def solution(mesh):

time: 124 us -> 123 us (level)
  local copies, waits for them, and re-layouts: 7.62 us -> 2.87 us
  Pallas kernels: 7.95 us -> 11.8 us
    unnamed x18 -> x10, local copies, waits for them, and re-layouts: 6.08 us -> 2 us
    ppermute x1, starting transfers between devices: 16.1 us -> 12.4 us  [local(): after = lax.ppermute(starts, SEQ, [(i + 1, i) for i in range(count - 1)])]
    ppermute x1, starting transfers between devices: 1.92 us -> 4.94 us  [local(): before = lax.ppermute(ends, SEQ, [(i, i + 1) for i in range(count - 1)])]
    pallas_call x1, Pallas kernels: 0.53 us -> 2.52 us  [local(): call(functools.partial(act_body, depth), (shape((length, width), BF), sha...]
    pallas_call x3 -> x4, Pallas kernels: 6.18 us -> 8.04 us  [the longest x1 4.32 us: local(): call(functools.partial(far_body, taps, depth), (shape((length, width), BF...]
  transfers between devices with their start and end apart: 5 -> 5, of which waited for: 2 -> 2; matrix products, arithmetic and copies ran while one was open for 1% -> 0% of each run, Pallas kernels for 1% -> 4%
where the time goes in v3:
time: 123 us
  blocking collectives  61.5 us (50%)
  starting transfers between devices  30.3 us (25%)
  waiting for transfers between devices  15.3 us (12%)
  Pallas kernels  11.8 us (10%)
  local copies, waits for them, and re-layouts  2.87 us (2%)
    all_to_all x1, blocking collectives, local(): lax.all_to_all(packed.transpose(1, 0, 2), 'z', 0, 0).transpose(1, 0, 2)  45.7 us
    all_to_all x1, blocking collectives, local(): own = lax.all_to_all(sent, XY, 0, 0)  15.8 us
    all_to_all x1, waiting for transfers between devices, local(): plane = lax.all_to_all(chip, XY, 0, 0)  13.9 us
    ppermute x1, starting transfers between devices, local(): after = lax.ppermute(starts, SEQ, [(i + 1, i) for i in range(count - 1)])  12.4 us
    ppermute x1, starting transfers between devices, local(): far = lax.ppermute(own, 'core', swap)  7.29 us
    ppermute x1, starting transfers between devices, local(): before = lax.ppermute(ends, SEQ, [(i, i + 1) for i in range(count - 1)])  4.94 us
    pallas_call x1, Pallas kernels, local(): call(functools.partial(far_body, taps, depth), (shape((length, width), BF...  4.32 us
    all_to_all x1, starting transfers between devices, local(): plane = lax.all_to_all(chip, XY, 0, 0)  3.74 us
  transfers between devices with their start and end apart: 5, of which 2 were waited for; matrix products, arithmetic and copies ran while one was open for 0% of the time, Pallas kernels for 4%

profile of v3, /device:TPU:1, one launch (start us, length us, event | category | flops | bytes accessed | tf_op | source)
XLA Modules:
  0.0 122.6 jit_solution(5084816779452647545)
XLA Ops:
  0.6 0.8 slice_bitcast_fusion
  1.4 4.9 %collective-permute-start = (bf16[4,384]{1,0:T(4,128)(2,1)S(1)}, bf16[4,384]{1,0:T(4,128)(2,1)S(1)}, u32[]{:S(2)}, u32[]{:S(2)}) collective-permute-start(bf16[4,384]{1,0:T(4,128)(2,1)S(1)} %pad_maximum_fusion), channel_id=1, source_target_pairs={{0,1},{1,2},{2,3},{3,4},{4,5},{5,6},{6,7},{7,8},{8,9},{9,10},{10,1... | collective-permute-start | bytes 9224 | tf_op jit(solution)/shard_map/ppermute | solution.py:249
  6.4 12.4 %collective-permute-start.1 = (bf16[4,384]{1,0:T(4,128)(2,1)S(1)}, bf16[4,384]{1,0:T(4,128)(2,1)S(1)}, u32[]{:S(2)}, u32[]{:S(2)}) collective-permute-start(bf16[4,384]{1,0:T(4,128)(2,1)S(1)} %pad_maximum_fusion.1), channel_id=1, source_target_pairs={{1,0},{2,1},{3,2},{4,3},{5,4},{6,5},{7,6},{8,7},{9,8},{10,9},{11,1... | collective-permute-start | bytes 9224 | tf_op jit(solution)/shard_map/ppermute | solution.py:250
  18.8 2.5 %shard_map.58 = (bf16[512,384]{1,0:T(8,128)(2,1)}, bf16[384,512]{1,0:T(8,128)(2,1)}) custom-call(s32[1]{0:T(128)} %bitcast.core_ref, bf16[512,384]{1,0:T(8,128)(2,1)} %bitcast.25, bf16[512,384]{1,0:T(8,128)(2,1)} %bitcast.28), custom_call_target="tpu_custom_call" | custom-call | flops 150994944 | bytes 1572864 | tf_op jit(solution)/shard_map/pallas_call | solution.py:254
  21.3 0.0 collective-permute-done.before_ref
  21.3 0.0 collective-permute-done.1.after_ref
  21.3 0.0 copy-start
  21.4 1.0 copy-done
  22.3 0.0 copy-start.1
  22.3 1.0 copy-done.1
  23.3 0.8 shard_map.60
  24.1 1.9 %collective-permute-start.2 = (bf16[15,64,384]{2,1,0:T(8,128)(2,1)S(1)}, bf16[15,64,384]{2,1,0:T(8,128)(2,1)S(1)}, u32[]{:S(2)}, u32[]{:S(2)}) collective-permute-start(bf16[15,64,384]{2,1,0:T(8,128)(2,1)S(1)} %shard_map.60), channel_id=1, source_target_pairs={{0,1},{1,0},{2,3},{3,2},{4,5},{5,4},{6,7},{7,6},{8,9},{9,8},{10,11... | collective-permute-start | bytes 2211848 | tf_op jit(solution)/shard_map/ppermute | solution.py:278
  26.1 0.8 shard_map.59.mine_ref
  26.8 1.4 %collective-permute-done.2.got_ref = bf16[15,64,384]{2,1,0:T(8,128)(2,1)S(1)} collective-permute-done((bf16[15,64,384]{2,1,0:T(8,128)(2,1)S(1)}, bf16[15,64,384]{2,1,0:T(8,128)(2,1)S(1)}, u32[]{:S(2)}, u32[]{:S(2)}) %collective-permute-start.2) | collective-permute-done | bytes 737312 | tf_op jit(solution)/shard_map/ppermute | solution.py:278
  28.2 1.0 shard_map.61
  29.3 0.0 copy-start.4
  29.3 3.7 %all-to-all-start = ((bf16[16,64,384]{2,1,0:T(8,128)(2,1)}), bf16[16,64,384]{2,1,0:T(8,128)(2,1)S(1)}, u32[]{:S(2)}, u32[]{:S(2)}) async-start(bf16[16,64,384]{2,1,0:T(8,128)(2,1)} %shard_map.61), calls=%async_computation | async-start | bytes 1572864 | tf_op jit(solution)/shard_map/all_to_all | solution.py:288
  33.0 0.0 copy-done.4
  33.1 13.9 %all-to-all-done.plane_ref = bf16[16,64,384]{2,1,0:T(8,128)(2,1)S(1)} async-done(((bf16[16,64,384]{2,1,0:T(8,128)(2,1)}), bf16[16,64,384]{2,1,0:T(8,128)(2,1)S(1)}, u32[]{:S(2)}, u32[]{:S(2)}) %all-to-all-start) | async-done | bytes 786464 | tf_op jit(solution)/shard_map/all_to_all | solution.py:288
  47.0 0.1 shard_map.62
  47.1 0.1 copy.6
  47.2 45.7 %all_to_all.15 = bf16[32,4,384]{2,1,0:T(4,128)(2,1)S(1)} all-to-all(bf16[32,4,384]{2,1,0:T(4,128)(2,1)S(1)} %copy.6), channel_id=1, replica_groups=mesh['x'=4,'y'=4,'z'=32,'core'=2] {'z'}, dimensions={0} | all-to-all | bytes 196608 | tf_op jit(solution)/shard_map/all_to_all | solution.py:300
  92.8 0.0 copy-start.2
  92.8 0.0 copy-start.3
  92.8 0.1 shard_map.63
  92.9 15.8 %all_to_all.16.own_ref = bf16[16,72,384]{2,1,0:T(8,128)(2,1)S(1)} all-to-all(bf16[16,72,384]{2,1,0:T(8,128)(2,1)S(1)} %shard_map.63), channel_id=1, replica_groups=mesh['x'=4,'y'=4,'z'=32,'core'=2] {'x','y'}, dimensions={0} | all-to-all | bytes 1769472 | tf_op jit(solution)/shard_map/all_to_all | solution.py:309
  108.8 7.3 %collective-permute-start.3 = (bf16[16,72,384]{2,1,0:T(8,128)(2,1)S(1)}, bf16[16,72,384]{2,1,0:T(8,128)(2,1)S(1)}, u32[]{:S(2)}, u32[]{:S(2)}) collective-permute-start(bf16[16,72,384]{2,1,0:T(8,128)(2,1)S(1)} %all_to_all.16.own_ref), channel_id=1, source_target_pairs={{0,1},{1,0},{2,3},{3,2},{4,5},{5,4},{6,7},{7,6},{8,9},{9,8},{10,11... | collective-permute-start | bytes 2654216 | tf_op jit(solution)/shard_map/ppermute | solution.py:310
  116.1 0.0 copy-done.2
  116.1 0.0 copy-done.3
  116.1 2.1 %shard_map.64 = (bf16[512,192]{1,0:T(8,128)(2,1)S(1)}, bf16[528,384]{1,0:T(8,128)(2,1)S(1)}, bf16[528,384]{1,0:T(8,128)(2,1)S(1)}, f32[5,6,384]{2,1,0:T(8,128)}) custom-call(s32[1]{0:T(128)} %bitcast.core_ref, bf16[512,384]{1,0:T(8,128)(2,1)S(1)} %bitcast.26, bf16[512,384]{1,0:T(8,128)(2,1)S(1)} %bitcast.29, ...), custom_call_target="tpu_custom_call" | custom-call | flops 754974720 | bytes 3145728 | tf_op jit(solution)/shard_map/pallas_call | solution.py:312
  118.2 0.0 collective-permute-done.3.far_ref
  118.2 4.3 %shard_map.65 = (bf16[512,384]{1,0:T(8,128)(2,1)}, bf16[512,384]{1,0:T(8,128)(2,1)}) custom-call(s32[1]{0:T(128)} %bitcast.core_ref, bf16[512,384]{1,0:T(8,128)(2,1)S(1)} %bitcast.27, bf16[512,384]{1,0:T(8,128)(2,1)S(1)} %bitcast.30, bf16[512,192]{1,0:T(8,128)(2,1)S(1)} %get-tuple-element.13.near_ref, bf16[528,384]{1,0:T(8,128)(2,1)S(1)} %get-tuple-element.14.act_ref, ...), custom_call_target="tpu_custom_call" | custom-call | flops 1509949440 | bytes 4718592 | tf_op jit(solution)/shard_map/pallas_call | solution.py:326
  (5 shorter events, 0.1 us)
Async XLA Ops:
  1.4 19.9 %collective-permute-start = (bf16[4,384]{1,0:T(4,128)(2,1)S(1)}, bf16[4,384]{1,0:T(4,128)(2,1)S(1)}, u32[]{:S(2)}, u32[]{:S(2)}) collective-permute-start(bf16[4,384]{1,0:T(4,128)(2,1)S(1)} %pad_maximum_fusion), channel_id=1, source_target_pairs={{0,1},{1,2},{2,3},{3,4},{4,5},{5,6},{6,7},{7,8},{8,9},{9,10},{10,1... | collective-permute-start | bytes 9224 | tf_op jit(solution)/shard_map/ppermute | solution.py:249
  6.4 15.0 %collective-permute-start.1 = (bf16[4,384]{1,0:T(4,128)(2,1)S(1)}, bf16[4,384]{1,0:T(4,128)(2,1)S(1)}, u32[]{:S(2)}, u32[]{:S(2)}) collective-permute-start(bf16[4,384]{1,0:T(4,128)(2,1)S(1)} %pad_maximum_fusion.1), channel_id=1, source_target_pairs={{1,0},{2,1},{3,2},{4,3},{5,4},{6,5},{7,6},{8,7},{9,8},{10,9},{11,1... | collective-permute-start | bytes 9224 | tf_op jit(solution)/shard_map/ppermute | solution.py:250
  21.3 1.0 copy-start
  22.3 1.0 copy-start.1
  24.1 4.1 %collective-permute-start.2 = (bf16[15,64,384]{2,1,0:T(8,128)(2,1)S(1)}, bf16[15,64,384]{2,1,0:T(8,128)(2,1)S(1)}, u32[]{:S(2)}, u32[]{:S(2)}) collective-permute-start(bf16[15,64,384]{2,1,0:T(8,128)(2,1)S(1)} %shard_map.60), channel_id=1, source_target_pairs={{0,1},{1,0},{2,3},{3,2},{4,5},{5,4},{6,7},{7,6},{8,9},{9,8},{10,11... | collective-permute-start | bytes 2211848 | tf_op jit(solution)/shard_map/ppermute | solution.py:278
  29.3 3.8 %copy-start.4 = (bf16[6,5,384]{2,0,1:T(8,128)(2,1)S(1)}, bf16[6,5,384]{2,0,1:T(8,128)(2,1)}, u32[]{:S(2)}) copy-start(bf16[6,5,384]{2,0,1:T(8,128)(2,1)} %param.4) | copy-start | bytes 69124
  29.3 17.7 %all-to-all-start = ((bf16[16,64,384]{2,1,0:T(8,128)(2,1)}), bf16[16,64,384]{2,1,0:T(8,128)(2,1)S(1)}, u32[]{:S(2)}, u32[]{:S(2)}) async-start(bf16[16,64,384]{2,1,0:T(8,128)(2,1)} %shard_map.61), calls=%async_computation | async-start | bytes 1572864 | tf_op jit(solution)/shard_map/all_to_all | solution.py:288
  92.8 23.3 %copy-start.2 = (bf16[1,512,384]{2,1,0:T(8,128)(2,1)S(1)}, bf16[1,512,384]{2,1,0:T(8,128)(2,1)}, u32[]{:S(2)}) copy-start(bf16[1,512,384]{2,1,0:T(8,128)(2,1)} %param.3) | copy-start | bytes 1179652
  92.8 23.3 %copy-start.3 = (bf16[1,512,384]{2,1,0:T(8,128)(2,1)S(1)}, bf16[1,512,384]{2,1,0:T(8,128)(2,1)}, u32[]{:S(2)}) copy-start(bf16[1,512,384]{2,1,0:T(8,128)(2,1)} %param.5) | copy-start | bytes 1179652
  108.8 9.5 %collective-permute-start.3 = (bf16[16,72,384]{2,1,0:T(8,128)(2,1)S(1)}, bf16[16,72,384]{2,1,0:T(8,128)(2,1)S(1)}, u32[]{:S(2)}, u32[]{:S(2)}) collective-permute-start(bf16[16,72,384]{2,1,0:T(8,128)(2,1)S(1)} %all_to_all.16.own_ref), channel_id=1, source_target_pairs={{0,1},{1,0},{2,3},{3,2},{4,5},{5,4},{6,7},{7,6},{8,9},{9,8},{10,11... | collective-permute-start | bytes 2654216 | tf_op jit(solution)/shard_map/ppermute | solution.py:310

commit v4 on v3

--- a/solution.py
+++ b/solution.py
@@ -13,13 +13,12 @@
 F32 = jnp.float32
 TOP = 8
 VMEM_BYTES = 24 * 1024 * 1024
-ALONE_BYTES = 63 * 1024 * 1024
-
-
-def call(body, out_shape, flops, bytes_accessed, scalars=0, plain=0, scratch=(), far=0, vmem=VMEM_BYTES):
+
+
+def call(body, out_shape, flops, bytes_accessed, scalars=0, plain=0, scratch=(), far=0):
     specs = [pl.BlockSpec(memory_space=pltpu.SMEM)] * scalars
     specs += [pl.BlockSpec(memory_space=pltpu.VMEM)] * plain
-    specs += [pl.BlockSpec(memory_space=pltpu.HBM)] * far
+    specs += [pl.BlockSpec(memory_space=pl.ANY)] * far
     outs = jax.tree.map(lambda _: pl.BlockSpec(memory_space=pltpu.VMEM), out_shape)
     return pl.pallas_call(
         body,
@@ -27,7 +26,7 @@
         in_specs=specs,
         out_specs=outs,
         scratch_shapes=list(scratch),
-        compiler_params=pltpu.CompilerParams(vmem_limit_bytes=vmem),
+        compiler_params=pltpu.CompilerParams(vmem_limit_bytes=VMEM_BYTES),
         cost_estimate=pl.CostEstimate(
             flops=flops, bytes_accessed=bytes_accessed, transcendentals=0
         ),
@@ -67,15 +66,9 @@
     return lax.dot_general(a, b, (((1,), (1,)), ((), ())), preferred_element_type=F32)
 
 
-def act_body(depth, core_ref, x_hbm, g_hbm, act_ref, cot_t_ref, x_ref, g_ref, sems):
-    get_g = pltpu.make_async_copy(g_hbm, g_ref, sems.at[0])
-    get_x = pltpu.make_async_copy(x_hbm, x_ref, sems.at[1])
-    get_g.start()
-    get_x.start()
+def act_body(depth, core_ref, x_ref, g_ref, act_ref, cot_t_ref):
     order = order_rows(core_ref[0], x_ref.shape[1], depth)
-    get_g.wait()
     cot_t_ref[...] = turn(order, g_ref[...]).astype(BF)
-    get_x.wait()
     act_ref[...] = gelu_rows(x_ref[...])
 
 
@@ -119,7 +112,8 @@
     out_ref[3] = total[depth:].astype(BF)
 
 
-def line_body(share, line_ref, out_ref):
+def line_body(share, line_ref, after_ref, out_ref):
+    del after_ref
     depth, width = line_ref.shape[1:]
     first = jnp.sum(line_ref[2].astype(F32), axis=0, keepdims=True) / share
     second = jnp.sum(line_ref[3].astype(F32), axis=0, keepdims=True) / share
@@ -136,39 +130,76 @@
     return jnp.concatenate([ref[shift * pairs + i, :rows] for i in range(pairs)], axis=0)
 
 
-def near_body(
-    taps,
+def prep_body(
     depth,
     core_ref,
     x_ref,
     g_ref,
     before_ref,
     after_ref,
-    own_ref,
-    near_ref,
+    packed_ref,
     act_ref,
     cot_ref,
-    kernel_grad_ref,
-    pad_ref,
+    slope_ref,
 ):
+    del packed_ref
     length, width = x_ref.shape
-    edge = (taps - 1) // 2
-    pairs = width // (4 * depth)
+    edge = before_ref.shape[0] // 2
     order = order_rows(core_ref[0], width, depth)
-    fill_act(pad_ref, gelu_rows(x_ref[...]), before_ref, after_ref, edge)
-    act_ref[...] = pad_ref[...].astype(BF)
-    total = jnp.zeros((length, width // 2), F32)
-    for shift in range(taps):
-        begin = TOP - edge + shift
-        window = pad_ref[begin : begin + length].astype(BF)
-        total = total + turn(window, weight(own_ref, shift, pairs, 2 * depth))
-    near_ref[...] = total.astype(BF)
+    zeros = jnp.zeros((TOP - edge, width), F32)
+    normed = norm(x_ref[...])[2]
+    share = cumulative(normed)
+    act_ref[TOP : TOP + length] = (normed * share).astype(BF)
+    first = gelu_rows(before_ref[:edge]).astype(F32)
+    last = gelu_rows(after_ref[:edge]).astype(F32)
+    act_ref[:TOP] = jnp.concatenate([zeros, first], axis=0).astype(BF)
+    act_ref[TOP + length :] = jnp.concatenate([last, zeros], axis=0).astype(BF)
     cot_ref[TOP : TOP + length] = turn(g_ref[...], order).astype(BF)
-    zeros = jnp.zeros((TOP - edge, width), F32)
     first = turn(before_ref[edge:], order)
     last = turn(after_ref[edge:], order)
     cot_ref[:TOP] = jnp.concatenate([zeros, first], axis=0).astype(BF)
     cot_ref[TOP + length :] = jnp.concatenate([last, zeros], axis=0).astype(BF)
+    slope_ref[...] = share + normed * jnp.exp(-0.5 * normed * normed) * 0.3989422804014327
+
+
+def half_convs(weights, act_pad_ref, cot_pad_ref, side, begin, rows):
+    taps = len(weights)
+    half, width = weights[0].shape
+    edge = (taps - 1) // 2
+    at = TOP - edge + begin
+    total = jnp.zeros((rows, half), F32)
+    carry = jnp.zeros((rows, width), F32)
+    for shift in range(taps):
+        window = act_pad_ref[at + shift : at + shift + rows].astype(BF)
+        total = total + turn(window, weights[shift])
+        back = at + 2 * edge - shift
+        window = cot_pad_ref[back : back + rows].astype(BF)[:, side * half : (side + 1) * half]
+        carry = carry + jnp.dot(window, weights[shift], preferred_element_type=F32)
+    return total.astype(BF), carry
+
+
+def near_body(
+    taps,
+    depth,
+    act_ref,
+    cot_ref,
+    own_ref,
+    near_ref,
+    carry_ref,
+    kernel_grad_ref,
+    act_pad_ref,
+    cot_pad_ref,
+):
+    length, half = near_ref.shape
+    pairs = half // (2 * depth)
+    act_pad_ref[...] = act_ref[...].astype(F32)
+    cot_pad_ref[...] = cot_ref[...].astype(F32)
+    own = [weight(own_ref, shift, pairs, 2 * depth) for shift in range(taps)]
+    rows = length // 2
+    for begin in range(0, length, rows):
+        near_ref[begin : begin + rows], carry_ref[begin : begin + rows] = half_convs(
+            own, act_pad_ref, cot_pad_ref, 0, begin, rows
+        )
     for shift in range(taps):
         for i in range(pairs):
             value = own_ref[shift * pairs + i, 2 * depth :].astype(F32)
@@ -181,10 +212,11 @@
     core_ref,
     x_ref,
     g_ref,
+    slope_ref,
     near_ref,
+    carry_ref,
     act_ref,
     cot_ref,
-    own_ref,
     far_ref,
     out_ref,
     grad_ref,
@@ -192,33 +224,20 @@
     cot_pad_ref,
 ):
     length, width = x_ref.shape
-    edge = (taps - 1) // 2
     pairs = width // (4 * depth)
     act_pad_ref[...] = act_ref[...].astype(F32)
     cot_pad_ref[...] = cot_ref[...].astype(F32)
     order = order_rows(core_ref[0], width, depth)
-    own = [weight(own_ref, shift, pairs, 2 * depth) for shift in range(taps)]
     far = [weight(far_ref, shift, pairs, 2 * depth) for shift in range(taps)]
     rows = length // 2
     for begin in range(0, length, rows):
-        at = TOP - edge + begin
-        total = jnp.zeros((rows, width // 2), F32)
-        carry = jnp.zeros((rows, width), F32)
-        for shift in range(taps):
-            back = at + 2 * edge - shift
-            window = cot_pad_ref[back : back + rows].astype(BF)
-            both = jnp.concatenate([own[shift], far[shift]], axis=0)
-            carry = carry + jnp.dot(window, both, preferred_element_type=F32)
-            window = act_pad_ref[at + shift : at + shift + rows].astype(BF)
-            total = total + turn(window, far[shift])
-        grouped = jnp.concatenate([near_ref[begin : begin + rows], total.astype(BF)], axis=1)
+        total, carry = half_convs(far, act_pad_ref, cot_pad_ref, 1, begin, rows)
+        carry = carry + carry_ref[begin : begin + rows]
+        grouped = jnp.concatenate([near_ref[begin : begin + rows], total], axis=1)
         branch = jnp.dot(grouped, order, preferred_element_type=F32)
         inputs, scale, normed = norm(x_ref[begin : begin + rows])
         out_ref[begin : begin + rows] = (inputs + branch).astype(BF)
-        slope = cumulative(normed) + normed * jnp.exp(-0.5 * normed * normed) * (
-            0.3989422804014327
-        )
-        normed_grad = carry * slope
+        normed_grad = carry * slope_ref[begin : begin + rows]
         project = jnp.mean(normed_grad * normed, axis=-1, keepdims=True)
         grad_ref[begin : begin + rows] = (
             g_ref[begin : begin + rows].astype(F32) + (normed_grad - normed * project) / scale
@@ -249,7 +268,6 @@
     before = lax.ppermute(ends, SEQ, [(i, i + 1) for i in range(count - 1)])
     after = lax.ppermute(starts, SEQ, [(i + 1, i) for i in range(count - 1)])
 
-    whole = pltpu.VMEM((length, width), BF)
     pad = pltpu.VMEM((padded, width), F32)
     act, cot_t = call(
         functools.partial(act_body, depth),
@@ -257,10 +275,7 @@
         2 * macs,
         4 * length * width * 2,
         1,
-        0,
-        [whole, whole, pltpu.SemaphoreType.DMA((2,))],
         2,
-        ALONE_BYTES,
     )(core, x, g)
     sides = [
         call(
@@ -297,6 +312,15 @@
         0,
         2,
     )(plane, rows)
+    act_rows, cot_rows, slope = call(
+        functools.partial(prep_body, depth),
+        (shape((padded, width), BF), shape((padded, width), BF), shape((length, width), F32)),
+        2 * macs,
+        8 * length * width * 2,
+        1,
+        4,
+        far=1,
+    )(core, x, g, before, after, packed)
     line = lax.all_to_all(packed.transpose(1, 0, 2), "z", 0, 0).transpose(1, 0, 2)
     sent = call(
         functools.partial(line_body, float(groups * section_input.shape[0])),
@@ -305,33 +329,33 @@
         groups * 2 * depth * width * 2,
         0,
         1,
-    )(line)
+        far=1,
+    )(line, act_rows)
     own = lax.all_to_all(sent, XY, 0, 0)
     far = lax.ppermute(own, "core", swap)
 
-    near, act_rows, cot_rows, kernel_grad = call(
+    near, carry, kernel_grad = call(
         functools.partial(near_body, taps, depth),
         (
             shape((length, half), BF),
-            shape((padded, width), BF),
-            shape((padded, width), BF),
+            shape((length, width), F32),
             shape((taps, held, width), F32),
         ),
         2 * taps * macs,
         8 * length * width * 2,
-        1,
-        5,
-        [pad],
-    )(core, x, g, before, after, own)
+        0,
+        3,
+        [pad, pad],
+    )(act_rows, cot_rows, own)
     out, grad = call(
         functools.partial(far_body, taps, depth),
         (shape((length, width), BF), shape((length, width), BF)),
-        4 * taps * macs,
+        2 * taps * macs,
         12 * length * width * 2,
         1,
-        7,
+        8,
         [pad, pad],
-    )(core, x, g, near, act_rows, cot_rows, own, far)
+    )(core, x, g, slope, near, carry, act_rows, cot_rows, far)
     return (out[None], grad[None], kernel_grad.transpose(1, 0, 2))
 
 

time: 123 us -> 121 us (0.984)
  blocking collectives: 61.5 us -> 15.8 us
  waiting for transfers between devices: 15.3 us -> 39.2 us
  starting transfers between devices: 30.3 us -> 51.2 us
  Pallas kernels: 11.8 us -> 9.62 us
    all_to_all x1 -> x0, blocking collectives: 45.7 us -> none  [local(): lax.all_to_all(packed.transpose(1, 0, 2), 'z', 0, 0).transpose(1, 0, 2)]
    all_to_all x0 -> x1, waiting for transfers between devices: none -> 24 us  [local(): lax.all_to_all(packed.transpose(1, 0, 2), 'z', 0, 0).transpose(1, 0, 2)]
    all_to_all x0 -> x1, starting transfers between devices: none -> 20.9 us  [local(): lax.all_to_all(packed.transpose(1, 0, 2), 'z', 0, 0).transpose(1, 0, 2)]
    pallas_call x1, Pallas kernels: 2.52 us -> 0.53 us  [local(): call(functools.partial(act_body, depth), (shape((length, width), BF), sha...]
  transfers between devices with their start and end apart: 5 -> 6, of which waited for: 2 -> 3; matrix products, arithmetic and copies ran while one was open for 0% -> 0% of each run, Pallas kernels for 4% -> 4%
where the time goes in v4:
time: 121 us; the launch traced here: 120 us
  starting transfers between devices  51.2 us (42%)
  waiting for transfers between devices  39.2 us (32%)
  blocking collectives  15.8 us (13%)
  Pallas kernels  9.62 us (8%)
  local copies, waits for them, and re-layouts  3.51 us (3%)
    all_to_all x1, waiting for transfers between devices, local(): lax.all_to_all(packed.transpose(1, 0, 2), 'z', 0, 0).transpose(1, 0, 2)  24 us
    all_to_all x1, starting transfers between devices, local(): lax.all_to_all(packed.transpose(1, 0, 2), 'z', 0, 0).transpose(1, 0, 2)  20.9 us
    all_to_all x1, blocking collectives, local(): own = lax.all_to_all(sent, XY, 0, 0)  15.8 us
    all_to_all x1, waiting for transfers between devices, local(): plane = lax.all_to_all(chip, XY, 0, 0)  13.9 us
    ppermute x1, starting transfers between devices, local(): after = lax.ppermute(starts, SEQ, [(i + 1, i) for i in range(count - 1)])  12.4 us
    ppermute x1, starting transfers between devices, local(): far = lax.ppermute(own, 'core', swap)  7.29 us
    ppermute x1, starting transfers between devices, local(): before = lax.ppermute(ends, SEQ, [(i, i + 1) for i in range(count - 1)])  4.94 us
    all_to_all x1, starting transfers between devices, local(): plane = lax.all_to_all(chip, XY, 0, 0)  3.74 us
  transfers between devices with their start and end apart: 6, of which 3 were waited for; matrix products, arithmetic and copies ran while one was open for 0% of the time, Pallas kernels for 4%

profile of v4, /device:TPU:1, one launch (start us, length us, event | category | flops | bytes accessed | tf_op | source)
XLA Modules:
  0.0 120.2 jit_solution(14332618764119001050)
XLA Ops:
  0.6 0.8 slice_bitcast_fusion
  1.4 4.9 %collective-permute-start = (bf16[4,384]{1,0:T(4,128)(2,1)S(1)}, bf16[4,384]{1,0:T(4,128)(2,1)S(1)}, u32[]{:S(2)}, u32[]{:S(2)}) collective-permute-start(bf16[4,384]{1,0:T(4,128)(2,1)S(1)} %pad_maximum_fusion), channel_id=1, source_target_pairs={{0,1},{1,2},{2,3},{3,4},{4,5},{5,6},{6,7},{7,8},{8,9},{9,10},{10,1... | collective-permute-start | bytes 9224 | tf_op jit(solution)/shard_map/ppermute | solution.py:268
  6.4 12.4 %collective-permute-start.1 = (bf16[4,384]{1,0:T(4,128)(2,1)S(1)}, bf16[4,384]{1,0:T(4,128)(2,1)S(1)}, u32[]{:S(2)}, u32[]{:S(2)}) collective-permute-start(bf16[4,384]{1,0:T(4,128)(2,1)S(1)} %pad_maximum_fusion.1), channel_id=1, source_target_pairs={{1,0},{2,1},{3,2},{4,3},{5,4},{6,5},{7,6},{8,7},{9,8},{10,9},{11,1... | collective-permute-start | bytes 9224 | tf_op jit(solution)/shard_map/ppermute | solution.py:269
  18.8 0.0 copy-start
  18.8 1.0 copy-done
  19.8 0.0 copy-start.2
  19.8 1.0 copy-done.2
  20.8 0.5 shard_map.58
  21.3 0.0 collective-permute-done.before_ref
  21.3 0.0 collective-permute-done.1.after_ref
  21.3 0.8 shard_map.60
  22.2 1.9 %collective-permute-start.2 = (bf16[15,64,384]{2,1,0:T(8,128)(2,1)S(1)}, bf16[15,64,384]{2,1,0:T(8,128)(2,1)S(1)}, u32[]{:S(2)}, u32[]{:S(2)}) collective-permute-start(bf16[15,64,384]{2,1,0:T(8,128)(2,1)S(1)} %shard_map.60), channel_id=1, source_target_pairs={{0,1},{1,0},{2,3},{3,2},{4,5},{5,4},{6,7},{7,6},{8,9},{9,8},{10,11... | collective-permute-start | bytes 2211848 | tf_op jit(solution)/shard_map/ppermute | solution.py:293
  24.1 0.8 shard_map.59.mine_ref
  24.9 1.4 %collective-permute-done.2.got_ref = bf16[15,64,384]{2,1,0:T(8,128)(2,1)S(1)} collective-permute-done((bf16[15,64,384]{2,1,0:T(8,128)(2,1)S(1)}, bf16[15,64,384]{2,1,0:T(8,128)(2,1)S(1)}, u32[]{:S(2)}, u32[]{:S(2)}) %collective-permute-start.2) | collective-permute-done | bytes 737312 | tf_op jit(solution)/shard_map/ppermute | solution.py:293
  26.3 1.0 shard_map.61
  27.3 0.0 copy-start.4
  27.3 0.0 copy-start.1
  27.3 0.0 copy-start.3
  27.3 3.7 %all-to-all-start = ((bf16[16,64,384]{2,1,0:T(8,128)(2,1)}), bf16[16,64,384]{2,1,0:T(8,128)(2,1)S(1)}, u32[]{:S(2)}, u32[]{:S(2)}) async-start(bf16[16,64,384]{2,1,0:T(8,128)(2,1)} %shard_map.61), calls=%async_computation | async-start | bytes 1572864 | tf_op jit(solution)/shard_map/all_to_all | solution.py:303
  31.1 0.0 copy-done.4
  31.2 13.9 %all-to-all-done.plane_ref = bf16[16,64,384]{2,1,0:T(8,128)(2,1)S(1)} async-done(((bf16[16,64,384]{2,1,0:T(8,128)(2,1)}), bf16[16,64,384]{2,1,0:T(8,128)(2,1)S(1)}, u32[]{:S(2)}, u32[]{:S(2)}) %all-to-all-start) | async-done | bytes 786464 | tf_op jit(solution)/shard_map/all_to_all | solution.py:303
  45.0 0.1 shard_map.62.packed_ref
  45.1 0.7 copy.6
  45.8 20.9 %all-to-all-start.1 = ((bf16[32,4,384]{2,1,0:T(4,128)(2,1)}), bf16[32,4,384]{2,1,0:T(4,128)(2,1)S(1)}, u32[]{:S(2)}, u32[]{:S(2)}) async-start(bf16[32,4,384]{2,1,0:T(4,128)(2,1)} %copy.6), calls=%async_computation.1 | async-start | bytes 196608 | tf_op jit(solution)/shard_map/all_to_all | solution.py:324
  66.8 0.0 copy-done.1
  66.8 0.0 copy-done.3
  66.8 0.9 shard_map.63
  67.7 24.0 %all-to-all-done.1 = bf16[32,4,384]{2,1,0:T(4,128)(2,1)S(1)} async-done(((bf16[32,4,384]{2,1,0:T(4,128)(2,1)}), bf16[32,4,384]{2,1,0:T(4,128)(2,1)S(1)}, u32[]{:S(2)}, u32[]{:S(2)}) %all-to-all-start.1) | async-done | bytes 98336 | tf_op jit(solution)/shard_map/all_to_all | solution.py:324
  91.7 0.1 shard_map.64
  91.8 15.8 %all_to_all.15.own_ref = bf16[16,72,384]{2,1,0:T(8,128)(2,1)S(1)} all-to-all(bf16[16,72,384]{2,1,0:T(8,128)(2,1)S(1)} %shard_map.64), channel_id=1, replica_groups=mesh['x'=4,'y'=4,'z'=32,'core'=2] {'x','y'}, dimensions={0} | all-to-all | bytes 1769472 | tf_op jit(solution)/shard_map/all_to_all | solution.py:334
  107.6 7.3 %collective-permute-start.3 = (bf16[16,72,384]{2,1,0:T(8,128)(2,1)S(1)}, bf16[16,72,384]{2,1,0:T(8,128)(2,1)S(1)}, u32[]{:S(2)}, u32[]{:S(2)}) collective-permute-start(bf16[16,72,384]{2,1,0:T(8,128)(2,1)S(1)} %all_to_all.15.own_ref), channel_id=1, source_target_pairs={{0,1},{1,0},{2,3},{3,2},{4,5},{5,4},{6,7},{7,6},{8,9},{9,8},{10,11... | collective-permute-start | bytes 2654216 | tf_op jit(solution)/shard_map/ppermute | solution.py:335
  114.9 2.1 %shard_map.65 = (bf16[512,192]{1,0:T(8,128)(2,1)S(1)}, f32[512,384]{1,0:T(8,128)S(1)}, f32[5,6,384]{2,1,0:T(8,128)}) custom-call(bf16[528,384]{1,0:T(8,128)(2,1)S(1)} %get-tuple-element.16.after_ref.act_ref, bf16[528,384]{1,0:T(8,128)(2,1)S(1)} %get-tuple-element.17.cot_ref, bf16[16,72,384]{2,1,0:T(8,128)(2,1)S(1)} %all_to_all.15.own_ref), custom_call_target="tpu_custom_call" | custom-call | flops 754974720 | bytes 3145728 | tf_op jit(solution)/shard_map/pallas_call | solution.py:337
  117.0 0.0 collective-permute-done.3.far_ref
  117.0 3.2 %shard_map.66 = (bf16[512,384]{1,0:T(8,128)(2,1)}, bf16[512,384]{1,0:T(8,128)(2,1)}) custom-call(s32[1]{0:T(128)} %bitcast.core_ref, bf16[512,384]{1,0:T(8,128)(2,1)S(1)} %bitcast.27, bf16[512,384]{1,0:T(8,128)(2,1)S(1)} %bitcast.30, f32[512,384]{1,0:T(8,128)S(1)} %get-tuple-element.15.slope_ref, bf16[512,192]{1,0:T(8,128)(2,1)S(1)} %get-tuple-element.18.near_ref, ...), custom_call_target="tpu_custom_call" | custom-call | flops 754974720 | bytes 4718592 | tf_op jit(solution)/shard_map/pallas_call | solution.py:350
  (5 shorter events, 0.1 us)
Async XLA Ops:
  1.4 19.9 %collective-permute-start = (bf16[4,384]{1,0:T(4,128)(2,1)S(1)}, bf16[4,384]{1,0:T(4,128)(2,1)S(1)}, u32[]{:S(2)}, u32[]{:S(2)}) collective-permute-start(bf16[4,384]{1,0:T(4,128)(2,1)S(1)} %pad_maximum_fusion), channel_id=1, source_target_pairs={{0,1},{1,2},{2,3},{3,4},{4,5},{5,6},{6,7},{7,8},{8,9},{9,10},{10,1... | collective-permute-start | bytes 9224 | tf_op jit(solution)/shard_map/ppermute | solution.py:268
  6.4 15.0 %collective-permute-start.1 = (bf16[4,384]{1,0:T(4,128)(2,1)S(1)}, bf16[4,384]{1,0:T(4,128)(2,1)S(1)}, u32[]{:S(2)}, u32[]{:S(2)}) collective-permute-start(bf16[4,384]{1,0:T(4,128)(2,1)S(1)} %pad_maximum_fusion.1), channel_id=1, source_target_pairs={{1,0},{2,1},{3,2},{4,3},{5,4},{6,5},{7,6},{8,7},{9,8},{10,9},{11,1... | collective-permute-start | bytes 9224 | tf_op jit(solution)/shard_map/ppermute | solution.py:269
  18.8 1.0 copy-start
  19.8 1.0 copy-start.2
  22.2 4.1 %collective-permute-start.2 = (bf16[15,64,384]{2,1,0:T(8,128)(2,1)S(1)}, bf16[15,64,384]{2,1,0:T(8,128)(2,1)S(1)}, u32[]{:S(2)}, u32[]{:S(2)}) collective-permute-start(bf16[15,64,384]{2,1,0:T(8,128)(2,1)S(1)} %shard_map.60), channel_id=1, source_target_pairs={{0,1},{1,0},{2,3},{3,2},{4,5},{5,4},{6,7},{7,6},{8,9},{9,8},{10,11... | collective-permute-start | bytes 2211848 | tf_op jit(solution)/shard_map/ppermute | solution.py:293
  27.3 3.8 %copy-start.4 = (bf16[6,5,384]{2,0,1:T(8,128)(2,1)S(1)}, bf16[6,5,384]{2,0,1:T(8,128)(2,1)}, u32[]{:S(2)}) copy-start(bf16[6,5,384]{2,0,1:T(8,128)(2,1)} %param.4) | copy-start | bytes 69124
  27.3 39.5 %copy-start.1 = (bf16[1,512,384]{2,1,0:T(8,128)(2,1)S(1)}, bf16[1,512,384]{2,1,0:T(8,128)(2,1)}, u32[]{:S(2)}) copy-start(bf16[1,512,384]{2,1,0:T(8,128)(2,1)} %param.3) | copy-start | bytes 1179652
  27.3 39.5 %copy-start.3 = (bf16[1,512,384]{2,1,0:T(8,128)(2,1)S(1)}, bf16[1,512,384]{2,1,0:T(8,128)(2,1)}, u32[]{:S(2)}) copy-start(bf16[1,512,384]{2,1,0:T(8,128)(2,1)} %param.5) | copy-start | bytes 1179652
  27.3 17.7 %all-to-all-start = ((bf16[16,64,384]{2,1,0:T(8,128)(2,1)}), bf16[16,64,384]{2,1,0:T(8,128)(2,1)S(1)}, u32[]{:S(2)}, u32[]{:S(2)}) async-start(bf16[16,64,384]{2,1,0:T(8,128)(2,1)} %shard_map.61), calls=%async_computation | async-start | bytes 1572864 | tf_op jit(solution)/shard_map/all_to_all | solution.py:303
  45.8 45.9 %all-to-all-start.1 = ((bf16[32,4,384]{2,1,0:T(4,128)(2,1)}), bf16[32,4,384]{2,1,0:T(4,128)(2,1)S(1)}, u32[]{:S(2)}, u32[]{:S(2)}) async-start(bf16[32,4,384]{2,1,0:T(4,128)(2,1)} %copy.6), calls=%async_computation.1 | async-start | bytes 196608 | tf_op jit(solution)/shard_map/all_to_all | solution.py:324
  107.6 9.4 %collective-permute-start.3 = (bf16[16,72,384]{2,1,0:T(8,128)(2,1)S(1)}, bf16[16,72,384]{2,1,0:T(8,128)(2,1)S(1)}, u32[]{:S(2)}, u32[]{:S(2)}) collective-permute-start(bf16[16,72,384]{2,1,0:T(8,128)(2,1)S(1)} %all_to_all.15.own_ref), channel_id=1, source_target_pairs={{0,1},{1,0},{2,3},{3,2},{4,5},{5,4},{6,7},{7,6},{8,9},{9,8},{10,11... | collective-permute-start | bytes 2654216 | tf_op jit(solution)/shard_map/ppermute | solution.py:335

commit v5 on v4

--- a/solution.py
+++ b/solution.py
@@ -66,26 +66,13 @@
     return lax.dot_general(a, b, (((1,), (1,)), ((), ())), preferred_element_type=F32)
 
 
-def act_body(depth, core_ref, x_ref, g_ref, act_ref, cot_t_ref):
-    order = order_rows(core_ref[0], x_ref.shape[1], depth)
-    cot_t_ref[...] = turn(order, g_ref[...]).astype(BF)
-    act_ref[...] = gelu_rows(x_ref[...])
-
-
-def fill_act(pad_ref, act, before_ref, after_ref, edge):
-    length = act.shape[0]
-    pad_ref[TOP - edge : TOP] = gelu_rows(before_ref[:edge]).astype(F32)
-    pad_ref[TOP : TOP + length] = act.astype(F32)
-    pad_ref[TOP + length : TOP + length + edge] = gelu_rows(after_ref[:edge]).astype(F32)
-
-
-def grad_body(taps, pairs, act_ref, cot_t_ref, before_ref, after_ref, out_ref, pad_ref, *, side):
+def local_grad(act_ref, cot_t, out_ref, pad_ref, taps, pairs):
     length, width = act_ref.shape
     edge = (taps - 1) // 2
-    half = width // 2
-    rows = half // pairs
-    fill_act(pad_ref, act_ref[...], before_ref, after_ref, edge)
-    cot_t = cot_t_ref[side * half : (side + 1) * half]
+    rows = cot_t.shape[0] // pairs
+    pad_ref[:TOP] = jnp.zeros((TOP, width), F32)
+    pad_ref[TOP : TOP + length] = act_ref[...].astype(F32)
+    pad_ref[TOP + length :] = jnp.zeros((TOP, width), F32)
     for shift in range(taps):
         begin = TOP - edge + shift
         window = pad_ref[begin : begin + length].astype(BF)
@@ -94,11 +81,79 @@
             out_ref[shift * pairs + i] = part[i * rows : (i + 1) * rows]
 
 
-def pair_body(mine_ref, got_ref, out_ref):
-    blocks = mine_ref.shape[0]
-    out_ref[:blocks] = (mine_ref[...] + got_ref[...].astype(F32)).astype(BF)
-    for extra in range(blocks, out_ref.shape[0]):
-        out_ref[extra] = jnp.zeros(out_ref.shape[1:], BF)
+def other_body(
+    taps,
+    pairs,
+    depth,
+    core_ref,
+    x_ref,
+    g_ref,
+    out_ref,
+    act_ref,
+    cot_t_ref,
+    starts_ref,
+    ends_ref,
+    pad_ref,
+):
+    length, width = x_ref.shape
+    half = width // 2
+    edge = (taps - 1) // 2
+    first = [ref[:TOP].astype(F32)[:edge] for ref in (x_ref, g_ref)]
+    last = [ref[length - TOP :].astype(F32)[TOP - edge :] for ref in (x_ref, g_ref)]
+    starts_ref[...] = jnp.concatenate(first, axis=0).astype(BF)
+    ends_ref[...] = jnp.concatenate(last, axis=0).astype(BF)
+    order = order_rows(core_ref[0], width, depth)
+    cot_t_ref[...] = turn(order, g_ref[...]).astype(BF)
+    act_ref[...] = gelu_rows(x_ref[...])
+    local_grad(act_ref, cot_t_ref[half:], out_ref, pad_ref, taps, pairs)
+
+
+def mine_body(taps, pairs, act_ref, cot_t_ref, out_ref, pad_ref):
+    half = cot_t_ref.shape[0] // 2
+    local_grad(act_ref, cot_t_ref[:half], out_ref, pad_ref, taps, pairs)
+
+
+def pair_body(
+    taps,
+    depth,
+    core_ref,
+    mine_ref,
+    got_ref,
+    before_ref,
+    starts_ref,
+    ends_ref,
+    after_ref,
+    out_ref,
+):
+    blocks, rows, width = mine_ref.shape
+    edge = (taps - 1) // 2
+    pairs = blocks // taps
+    half = width // 2
+    parts = [ref[...].astype(F32) for ref in (before_ref, starts_ref, ends_ref, after_ref)]
+    act = gelu_rows(jnp.concatenate([p[:edge] for p in parts], axis=0)).astype(F32)
+    cot = jnp.concatenate([p[edge:] for p in parts], axis=0).astype(BF)
+    order = order_rows(core_ref[0], width, depth)
+    cot_t = turn(order, cot)[:half].astype(BF)
+    side = 2 * edge
+    for shift in range(taps):
+        offset = shift - edge
+        window = []
+        for i in range(2 * side):
+            at = i % side
+            to = at + offset
+            crosses = 0 <= to < side and (at < edge) != (to < edge)
+            row = i + offset
+            window.append(act[row : row + 1] if crosses else jnp.zeros((1, width), F32))
+        extra = jnp.dot(
+            cot_t, jnp.concatenate(window, axis=0).astype(BF), preferred_element_type=F32
+        )
+        for i in range(pairs):
+            j = shift * pairs + i
+            out_ref[j] = (
+                mine_ref[j] + got_ref[j].astype(F32) + extra[i * rows : (i + 1) * rows]
+            ).astype(BF)
+    for j in range(blocks, out_ref.shape[0]):
+        out_ref[j] = jnp.zeros((rows, width), BF)
 
 
 def plane_body(depth, plane_ref, row_ref, out_ref):
@@ -167,11 +222,10 @@
     half, width = weights[0].shape
     edge = (taps - 1) // 2
     at = TOP - edge + begin
-    total = jnp.zeros((rows, half), F32)
+    windows = [act_pad_ref[at + shift : at + shift + rows].astype(BF) for shift in range(taps)]
+    total = turn(jnp.concatenate(windows, axis=1), jnp.concatenate(weights, axis=1))
     carry = jnp.zeros((rows, width), F32)
     for shift in range(taps):
-        window = act_pad_ref[at + shift : at + shift + rows].astype(BF)
-        total = total + turn(window, weights[shift])
         back = at + 2 * edge - shift
         window = cot_pad_ref[back : back + rows].astype(BF)[:, side * half : (side + 1) * half]
         carry = carry + jnp.dot(window, weights[shift], preferred_element_type=F32)
@@ -263,43 +317,38 @@
     swap = [(0, 1), (1, 0)]
     macs = length * width * width
 
-    ends = jnp.concatenate([x[length - edge :], g[length - edge :]], axis=0)
-    starts = jnp.concatenate([x[:edge], g[:edge]], axis=0)
+    pad = pltpu.VMEM((padded, width), F32)
+    block = (blocks, 2 * depth, width)
+    rim = shape((2 * edge, width), BF)
+    other, act, cot_t, starts, ends = call(
+        functools.partial(other_body, taps, pairs, depth),
+        (shape(block, BF), shape((length, width), BF), shape((width, length), BF), rim, rim),
+        2 * macs + taps * macs,
+        8 * length * width * 2,
+        1,
+        2,
+        [pad],
+    )(core, x, g)
+    got = lax.ppermute(other, "core", swap)
     before = lax.ppermute(ends, SEQ, [(i, i + 1) for i in range(count - 1)])
     after = lax.ppermute(starts, SEQ, [(i + 1, i) for i in range(count - 1)])
-
-    pad = pltpu.VMEM((padded, width), F32)
-    act, cot_t = call(
-        functools.partial(act_body, depth),
-        (shape((length, width), BF), shape((width, length), BF)),
-        2 * macs,
-        4 * length * width * 2,
-        1,
+    mine = call(
+        functools.partial(mine_body, taps, pairs),
+        shape(block, F32),
+        taps * macs,
+        8 * length * width * 2,
+        0,
         2,
-    )(core, x, g)
-    sides = [
-        call(
-            functools.partial(grad_body, taps, pairs, side=side),
-            shape((blocks, 2 * depth, width), kind),
-            taps * macs,
-            8 * length * width * 2,
-            0,
-            4,
-            [pad],
-        )
-        for side, kind in ((0, F32), (1, BF))
-    ]
-    other = sides[1](act, cot_t, before, after)
-    got = lax.ppermute(other, "core", swap)
-    mine = sides[0](act, cot_t, before, after)
+        [pad],
+    )(act, cot_t)
     chip = call(
-        pair_body,
+        functools.partial(pair_body, taps, depth),
         shape((groups, 2 * depth, width), BF),
         taps * half * width,
         taps * half * width * 8,
-        0,
-        2,
-    )(mine, got)
+        1,
+        6,
+    )(core, mine, got, before, starts, ends, after)
     plane = lax.all_to_all(chip, XY, 0, 0)
 
     by_block = kernel.reshape(pairs, 2, taps, width).transpose(2, 0, 1, 3).reshape(blocks, 2, width)

time: 121 us -> 120 us (level)
  waiting for transfers between devices: 39.2 us -> 41.2 us
  blocking collectives: 15.8 us -> 14 us
    ppermute x1, starting transfers between devices: 1.92 us -> 16.1 us  [local(): got = lax.ppermute(other, 'core', swap)]
    ppermute x1, starting transfers between devices: 12.4 us -> 2.4 us  [local(): after = lax.ppermute(starts, SEQ, [(i + 1, i) for i in range(count - 1)])]
    ppermute x1, starting transfers between devices: 4.94 us -> 1.92 us  [local(): before = lax.ppermute(ends, SEQ, [(i, i + 1) for i in range(count - 1)])]
    all_to_all x1, blocking collectives: 15.8 us -> 14 us  [local(): own = lax.all_to_all(sent, XY, 0, 0)]
    ppermute x1, waiting for transfers between devices: 0.01 us -> 1.78 us  [local(): after = lax.ppermute(starts, SEQ, [(i + 1, i) for i in range(count - 1)])]
    all_to_all x1, waiting for transfers between devices: 24 us -> 25.5 us  [local(): lax.all_to_all(packed.transpose(1, 0, 2), 'z', 0, 0).transpose(1, 0, 2)]
    ppermute x1, waiting for transfers between devices: 1.36 us -> 0.01 us  [local(): got = lax.ppermute(other, 'core', swap)]
    pallas_call x4 -> x3, Pallas kernels: 3.19 us -> 3.32 us  [the longest x1 1.37 us: local(): call(functools.partial(pair_body, taps, depth), shape((groups, 2 * depth,...]
  transfers between devices with their start and end apart: 6 -> 6, of which waited for: 3 -> 3; matrix products, arithmetic and copies ran while one was open for 0% -> 0% of each run, Pallas kernels for 4% -> 3%
where the time goes in v5:
time: 120 us; the launch traced here: 119 us
  starting transfers between devices  51.1 us (43%)
  waiting for transfers between devices  41.2 us (34%)
  blocking collectives  14 us (12%)
  Pallas kernels  9.37 us (8%)
  local copies, waits for them, and re-layouts  2.76 us (2%)
    all_to_all x1, waiting for transfers between devices, local(): lax.all_to_all(packed.transpose(1, 0, 2), 'z', 0, 0).transpose(1, 0, 2)  25.5 us
    all_to_all x1, starting transfers between devices, local(): lax.all_to_all(packed.transpose(1, 0, 2), 'z', 0, 0).transpose(1, 0, 2)  20.1 us
    ppermute x1, starting transfers between devices, local(): got = lax.ppermute(other, 'core', swap)  16.1 us
    all_to_all x1, blocking collectives, local(): own = lax.all_to_all(sent, XY, 0, 0)  14 us
    all_to_all x1, waiting for transfers between devices, local(): plane = lax.all_to_all(chip, XY, 0, 0)  13.9 us
    ppermute x1, starting transfers between devices, local(): far = lax.ppermute(own, 'core', swap)  6.84 us
    all_to_all x1, starting transfers between devices, local(): plane = lax.all_to_all(chip, XY, 0, 0)  3.74 us
    pallas_call x1, Pallas kernels, local(): call(functools.partial(far_body, taps, depth), (shape((length, width), BF...  2.97 us
  transfers between devices with their start and end apart: 6, of which 3 were waited for; matrix products, arithmetic and copies ran while one was open for 0% of the time, Pallas kernels for 3%

profile of v5, /device:TPU:1, one launch (start us, length us, event | category | flops | bytes accessed | tf_op | source)
XLA Modules:
  0.0 119.1 jit_solution(10842388653140243626)
XLA Ops:
  0.6 0.0 copy-start
  0.6 1.0 copy-done
  1.6 0.0 copy-start.2
  1.6 1.0 copy-done.2
  2.6 1.2 %shard_map.58 = (bf16[15,64,384]{2,1,0:T(8,128)(2,1)S(1)}, bf16[512,384]{1,0:T(8,128)(2,1)S(1)}, bf16[384,512]{1,0:T(8,128)(2,1)S(1)}, bf16[4,384]{1,0:T(4,128)(2,1)S(1)}, bf16[4,384]{1,0:T(4,128)(2,1)S(1)}) custom-call(s32[1]{0:T(128)} %bitcast.core_ref, bf16[512,384]{1,0:T(8,128)(2,1)S(1)} %bitcast.17, bf16[512,384]{1,0:T(8,128)(2,1)S(1)} %bitcast.20), custom_call_target="tpu_custom_call" | custom-call | flops 528482304 | bytes 3145728 | tf_op jit(solution)/shard_map/pallas_call | solution.py:323
  3.9 16.1 %collective-permute-start.2 = (bf16[15,64,384]{2,1,0:T(8,128)(2,1)S(1)}, bf16[15,64,384]{2,1,0:T(8,128)(2,1)S(1)}, u32[]{:S(2)}, u32[]{:S(2)}) collective-permute-start(bf16[15,64,384]{2,1,0:T(8,128)(2,1)S(1)} %get-tuple-element.20), channel_id=1, source_target_pairs={{0,1},{1,0},{2,3},{3,2},{4,5},{5,4},{6,7},{7,6},{8,9},{9,8},{10,11... | collective-permute-start | bytes 2211848 | tf_op jit(solution)/shard_map/ppermute | solution.py:332
  19.9 1.9 %collective-permute-start = (bf16[4,384]{1,0:T(4,128)(2,1)S(1)}, bf16[4,384]{1,0:T(4,128)(2,1)S(1)}, u32[]{:S(2)}, u32[]{:S(2)}) collective-permute-start(bf16[4,384]{1,0:T(4,128)(2,1)S(1)} %get-tuple-element.16.ends_ref), channel_id=1, source_target_pairs={{0,1},{1,2},{2,3},{3,4},{4,5},{5,6},{6,7},{7,8},{8,9},{9,10},{10,1... | collective-permute-start | bytes 9224 | tf_op jit(solution)/shard_map/ppermute | solution.py:333
  21.9 2.4 %collective-permute-start.1 = (bf16[4,384]{1,0:T(4,128)(2,1)S(1)}, bf16[4,384]{1,0:T(4,128)(2,1)S(1)}, u32[]{:S(2)}, u32[]{:S(2)}) collective-permute-start(bf16[4,384]{1,0:T(4,128)(2,1)S(1)} %get-tuple-element.17.starts_ref), channel_id=1, source_target_pairs={{1,0},{2,1},{3,2},{4,3},{5,4},{6,5},{7,6},{8,7},{9,8},{10,9},{11,1... | collective-permute-start | bytes 9224 | tf_op jit(solution)/shard_map/ppermute | solution.py:334
  24.3 0.7 shard_map.59.mine_ref
  25.0 0.0 collective-permute-done.before_ref
  25.0 1.8 %collective-permute-done.1.after_ref = bf16[4,384]{1,0:T(4,128)(2,1)S(1)} collective-permute-done((bf16[4,384]{1,0:T(4,128)(2,1)S(1)}, bf16[4,384]{1,0:T(4,128)(2,1)S(1)}, u32[]{:S(2)}, u32[]{:S(2)}) %collective-permute-start.1) | collective-permute-done | bytes 3104 | tf_op jit(solution)/shard_map/ppermute | solution.py:334
  26.8 0.0 collective-permute-done.2.got_ref
  26.8 1.4 %shard_map.60 = bf16[16,64,384]{2,1,0:T(8,128)(2,1)} custom-call(s32[1]{0:T(128)} %bitcast.core_ref, f32[15,64,384]{2,1,0:T(8,128)S(1)} %shard_map.59.mine_ref, bf16[15,64,384]{2,1,0:T(8,128)(2,1)S(1)} %collective-permute-done.2.got_ref, bf16[4,384]{1,0:T(4,128)(2,1)S(1)} %collective-permute-done.before_ref, ...), custom_call_target="tpu_custom_call" | custom-call | flops 368640 | bytes 2949120 | tf_op jit(solution)/shard_map/pallas_call | solution.py:344
  28.2 0.0 copy-start.4
  28.2 0.0 copy-start.1
  28.2 0.0 copy-start.3
  28.2 3.7 %all-to-all-start = ((bf16[16,64,384]{2,1,0:T(8,128)(2,1)}), bf16[16,64,384]{2,1,0:T(8,128)(2,1)S(1)}, u32[]{:S(2)}, u32[]{:S(2)}) async-start(bf16[16,64,384]{2,1,0:T(8,128)(2,1)} %shard_map.60), calls=%async_computation | async-start | bytes 1572864 | tf_op jit(solution)/shard_map/all_to_all | solution.py:352
  31.9 0.0 copy-done.4
  32.0 13.9 %all-to-all-done.plane_ref = bf16[16,64,384]{2,1,0:T(8,128)(2,1)S(1)} async-done(((bf16[16,64,384]{2,1,0:T(8,128)(2,1)}), bf16[16,64,384]{2,1,0:T(8,128)(2,1)S(1)}, u32[]{:S(2)}, u32[]{:S(2)}) %all-to-all-start) | async-done | bytes 786464 | tf_op jit(solution)/shard_map/all_to_all | solution.py:352
  45.9 0.1 shard_map.61.packed_ref
  46.0 0.7 copy.6
  46.7 20.1 %all-to-all-start.1 = ((bf16[32,4,384]{2,1,0:T(4,128)(2,1)}), bf16[32,4,384]{2,1,0:T(4,128)(2,1)S(1)}, u32[]{:S(2)}, u32[]{:S(2)}) async-start(bf16[32,4,384]{2,1,0:T(4,128)(2,1)} %copy.6), calls=%async_computation.1 | async-start | bytes 196608 | tf_op jit(solution)/shard_map/all_to_all | solution.py:373
  66.8 0.0 copy-done.1
  66.8 0.0 copy-done.3
  66.8 0.9 shard_map.62
  67.7 25.5 %all-to-all-done.1 = bf16[32,4,384]{2,1,0:T(4,128)(2,1)S(1)} async-done(((bf16[32,4,384]{2,1,0:T(4,128)(2,1)}), bf16[32,4,384]{2,1,0:T(4,128)(2,1)S(1)}, u32[]{:S(2)}, u32[]{:S(2)}) %all-to-all-start.1) | async-done | bytes 98336 | tf_op jit(solution)/shard_map/all_to_all | solution.py:373
  93.2 0.1 shard_map.63
  93.3 14.0 %all_to_all.15.own_ref = bf16[16,72,384]{2,1,0:T(8,128)(2,1)S(1)} all-to-all(bf16[16,72,384]{2,1,0:T(8,128)(2,1)S(1)} %shard_map.63), channel_id=1, replica_groups=mesh['x'=4,'y'=4,'z'=32,'core'=2] {'x','y'}, dimensions={0} | all-to-all | bytes 1769472 | tf_op jit(solution)/shard_map/all_to_all | solution.py:383
  107.3 6.8 %collective-permute-start.3 = (bf16[16,72,384]{2,1,0:T(8,128)(2,1)S(1)}, bf16[16,72,384]{2,1,0:T(8,128)(2,1)S(1)}, u32[]{:S(2)}, u32[]{:S(2)}) collective-permute-start(bf16[16,72,384]{2,1,0:T(8,128)(2,1)S(1)} %all_to_all.15.own_ref), channel_id=1, source_target_pairs={{0,1},{1,0},{2,3},{3,2},{4,5},{5,4},{6,7},{7,6},{8,9},{9,8},{10,11... | collective-permute-start | bytes 2654216 | tf_op jit(solution)/shard_map/ppermute | solution.py:384
  114.1 2.0 %shard_map.64 = (bf16[512,192]{1,0:T(8,128)(2,1)S(1)}, f32[512,384]{1,0:T(8,128)S(1)}, f32[5,6,384]{2,1,0:T(8,128)}) custom-call(bf16[528,384]{1,0:T(8,128)(2,1)S(1)} %get-tuple-element.22.after_ref.act_ref, bf16[528,384]{1,0:T(8,128)(2,1)S(1)} %get-tuple-element.23.cot_ref, bf16[16,72,384]{2,1,0:T(8,128)(2,1)S(1)} %all_to_all.15.own_ref), custom_call_target="tpu_custom_call" | custom-call | flops 754974720 | bytes 3145728 | tf_op jit(solution)/shard_map/pallas_call | solution.py:386
  116.1 0.0 collective-permute-done.3.far_ref
  116.2 3.0 %shard_map.65 = (bf16[512,384]{1,0:T(8,128)(2,1)}, bf16[512,384]{1,0:T(8,128)(2,1)}) custom-call(s32[1]{0:T(128)} %bitcast.core_ref, bf16[512,384]{1,0:T(8,128)(2,1)S(1)} %bitcast.19, bf16[512,384]{1,0:T(8,128)(2,1)S(1)} %bitcast.22, f32[512,384]{1,0:T(8,128)S(1)} %get-tuple-element.21.slope_ref, bf16[512,192]{1,0:T(8,128)(2,1)S(1)} %get-tuple-element.24.near_ref, ...), custom_call_target="tpu_custom_call" | custom-call | flops 754974720 | bytes 4718592 | tf_op jit(solution)/shard_map/pallas_call | solution.py:399
  (3 shorter events, 0.1 us)
Async XLA Ops:
  0.6 1.0 copy-start
  1.6 1.0 copy-start.2
  3.9 22.9 %collective-permute-start.2 = (bf16[15,64,384]{2,1,0:T(8,128)(2,1)S(1)}, bf16[15,64,384]{2,1,0:T(8,128)(2,1)S(1)}, u32[]{:S(2)}, u32[]{:S(2)}) collective-permute-start(bf16[15,64,384]{2,1,0:T(8,128)(2,1)S(1)} %get-tuple-element.20), channel_id=1, source_target_pairs={{0,1},{1,0},{2,3},{3,2},{4,5},{5,4},{6,7},{7,6},{8,9},{9,8},{10,11... | collective-permute-start | bytes 2211848 | tf_op jit(solution)/shard_map/ppermute | solution.py:332
  19.9 5.1 %collective-permute-start = (bf16[4,384]{1,0:T(4,128)(2,1)S(1)}, bf16[4,384]{1,0:T(4,128)(2,1)S(1)}, u32[]{:S(2)}, u32[]{:S(2)}) collective-permute-start(bf16[4,384]{1,0:T(4,128)(2,1)S(1)} %get-tuple-element.16.ends_ref), channel_id=1, source_target_pairs={{0,1},{1,2},{2,3},{3,4},{4,5},{5,6},{6,7},{7,8},{8,9},{9,10},{10,1... | collective-permute-start | bytes 9224 | tf_op jit(solution)/shard_map/ppermute | solution.py:333
  21.9 4.9 %collective-permute-start.1 = (bf16[4,384]{1,0:T(4,128)(2,1)S(1)}, bf16[4,384]{1,0:T(4,128)(2,1)S(1)}, u32[]{:S(2)}, u32[]{:S(2)}) collective-permute-start(bf16[4,384]{1,0:T(4,128)(2,1)S(1)} %get-tuple-element.17.starts_ref), channel_id=1, source_target_pairs={{1,0},{2,1},{3,2},{4,3},{5,4},{6,5},{7,6},{8,7},{9,8},{10,9},{11,1... | collective-permute-start | bytes 9224 | tf_op jit(solution)/shard_map/ppermute | solution.py:334
  28.2 3.8 %copy-start.4 = (bf16[6,5,384]{2,0,1:T(8,128)(2,1)S(1)}, bf16[6,5,384]{2,0,1:T(8,128)(2,1)}, u32[]{:S(2)}) copy-start(bf16[6,5,384]{2,0,1:T(8,128)(2,1)} %param.4) | copy-start | bytes 69124
  28.2 38.6 %copy-start.1 = (bf16[1,512,384]{2,1,0:T(8,128)(2,1)S(1)}, bf16[1,512,384]{2,1,0:T(8,128)(2,1)}, u32[]{:S(2)}) copy-start(bf16[1,512,384]{2,1,0:T(8,128)(2,1)} %param.3) | copy-start | bytes 1179652
  28.2 38.7 %copy-start.3 = (bf16[1,512,384]{2,1,0:T(8,128)(2,1)S(1)}, bf16[1,512,384]{2,1,0:T(8,128)(2,1)}, u32[]{:S(2)}) copy-start(bf16[1,512,384]{2,1,0:T(8,128)(2,1)} %param.5) | copy-start | bytes 1179652
  28.2 17.7 %all-to-all-start = ((bf16[16,64,384]{2,1,0:T(8,128)(2,1)}), bf16[16,64,384]{2,1,0:T(8,128)(2,1)S(1)}, u32[]{:S(2)}, u32[]{:S(2)}) async-start(bf16[16,64,384]{2,1,0:T(8,128)(2,1)} %shard_map.60), calls=%async_computation | async-start | bytes 1572864 | tf_op jit(solution)/shard_map/all_to_all | solution.py:352
  46.7 46.6 %all-to-all-start.1 = ((bf16[32,4,384]{2,1,0:T(4,128)(2,1)}), bf16[32,4,384]{2,1,0:T(4,128)(2,1)S(1)}, u32[]{:S(2)}, u32[]{:S(2)}) async-start(bf16[32,4,384]{2,1,0:T(4,128)(2,1)} %copy.6), calls=%async_computation.1 | async-start | bytes 196608 | tf_op jit(solution)/shard_map/all_to_all | solution.py:373
  107.3 8.9 %collective-permute-start.3 = (bf16[16,72,384]{2,1,0:T(8,128)(2,1)S(1)}, bf16[16,72,384]{2,1,0:T(8,128)(2,1)S(1)}, u32[]{:S(2)}, u32[]{:S(2)}) collective-permute-start(bf16[16,72,384]{2,1,0:T(8,128)(2,1)S(1)} %all_to_all.15.own_ref), channel_id=1, source_target_pairs={{0,1},{1,0},{2,3},{3,2},{4,5},{5,4},{6,7},{7,6},{8,9},{9,8},{10,11... | collective-permute-start | bytes 2654216 | tf_op jit(solution)/shard_map/ppermute | solution.py:384

commit v6 on v5

--- a/solution.py
+++ b/solution.py
@@ -93,6 +93,7 @@
     cot_t_ref,
     starts_ref,
     ends_ref,
+    outer_ref,
     pad_ref,
 ):
     length, width = x_ref.shape
@@ -100,8 +101,15 @@
     edge = (taps - 1) // 2
     first = [ref[:TOP].astype(F32)[:edge] for ref in (x_ref, g_ref)]
     last = [ref[length - TOP :].astype(F32)[TOP - edge :] for ref in (x_ref, g_ref)]
-    starts_ref[...] = jnp.concatenate(first, axis=0).astype(BF)
-    ends_ref[...] = jnp.concatenate(last, axis=0).astype(BF)
+    first = jnp.concatenate(first, axis=0)
+    last = jnp.concatenate(last, axis=0)
+    starts_ref[...] = first.astype(BF)
+    ends_ref[...] = last.astype(BF)
+    left = core_ref[0] == 0
+    outer_ref[...] = jnp.where(left, first, last).astype(BF)
+    inner = jnp.where(left, last, first)
+    rest = jnp.zeros((out_ref.shape[1] - first.shape[0], width), F32)
+    out_ref[taps * pairs] = jnp.concatenate([inner, rest], axis=0).astype(BF)
     order = order_rows(core_ref[0], width, depth)
     cot_t_ref[...] = turn(order, g_ref[...]).astype(BF)
     act_ref[...] = gelu_rows(x_ref[...])
@@ -119,17 +127,25 @@
     core_ref,
     mine_ref,
     got_ref,
-    before_ref,
+    outer_ref,
     starts_ref,
     ends_ref,
+    out_ref,
+    before_ref,
     after_ref,
-    out_ref,
 ):
     blocks, rows, width = mine_ref.shape
     edge = (taps - 1) // 2
     pairs = blocks // taps
     half = width // 2
-    parts = [ref[...].astype(F32) for ref in (before_ref, starts_ref, ends_ref, after_ref)]
+    left = core_ref[0] == 0
+    outer = outer_ref[...].astype(F32)
+    inner = got_ref[blocks].astype(F32)[: 2 * edge]
+    before = jnp.where(left, outer, inner)
+    after = jnp.where(left, inner, outer)
+    before_ref[...] = before.astype(BF)
+    after_ref[...] = after.astype(BF)
+    parts = [before, starts_ref[...].astype(F32), ends_ref[...].astype(F32), after]
     act = gelu_rows(jnp.concatenate([p[:edge] for p in parts], axis=0)).astype(F32)
     cot = jnp.concatenate([p[edge:] for p in parts], axis=0).astype(BF)
     order = order_rows(core_ref[0], width, depth)
@@ -320,9 +336,16 @@
     pad = pltpu.VMEM((padded, width), F32)
     block = (blocks, 2 * depth, width)
     rim = shape((2 * edge, width), BF)
-    other, act, cot_t, starts, ends = call(
+    other, act, cot_t, starts, ends, outer = call(
         functools.partial(other_body, taps, pairs, depth),
-        (shape(block, BF), shape((length, width), BF), shape((width, length), BF), rim, rim),
+        (
+            shape((blocks + 1, 2 * depth, width), BF),
+            shape((length, width), BF),
+            shape((width, length), BF),
+            rim,
+            rim,
+            rim,
+        ),
         2 * macs + taps * macs,
         8 * length * width * 2,
         1,
@@ -330,8 +353,8 @@
         [pad],
     )(core, x, g)
     got = lax.ppermute(other, "core", swap)
-    before = lax.ppermute(ends, SEQ, [(i, i + 1) for i in range(count - 1)])
-    after = lax.ppermute(starts, SEQ, [(i + 1, i) for i in range(count - 1)])
+    across = [(i, i + 1) for i in range(1, count - 1, 2)]
+    outer = lax.ppermute(outer, SEQ, across + [(j, i) for i, j in across])
     mine = call(
         functools.partial(mine_body, taps, pairs),
         shape(block, F32),
@@ -341,14 +364,14 @@
         2,
         [pad],
     )(act, cot_t)
-    chip = call(
+    chip, before, after = call(
         functools.partial(pair_body, taps, depth),
-        shape((groups, 2 * depth, width), BF),
+        (shape((groups, 2 * depth, width), BF), rim, rim),
         taps * half * width,
         taps * half * width * 8,
         1,
-        6,
-    )(core, mine, got, before, starts, ends, after)
+        5,
+    )(core, mine, got, outer, starts, ends)
     plane = lax.all_to_all(chip, XY, 0, 0)
 
     by_block = kernel.reshape(pairs, 2, taps, width).transpose(2, 0, 1, 3).reshape(blocks, 2, width)

time: 120 us -> 117 us (0.975)
  waiting for transfers between devices: 41.2 us -> 39.9 us
    ppermute x2 -> x1, starting transfers between devices: 4.32 us -> 1.92 us  [local(): outer = lax.ppermute(outer, SEQ, across + [(j, i) for i, j in across])]
    all_to_all x1, waiting for transfers between devices: 13.9 us -> 12.2 us  [local(): plane = lax.all_to_all(chip, XY, 0, 0)]
  transfers between devices with their start and end apart: 6 -> 5, of which waited for: 3 -> 3; matrix products, arithmetic and copies ran while one was open for 0% -> 0% of each run, Pallas kernels for 3% -> 3%
where the time goes in v6:
time: 117 us; the launch traced here: 116 us
  starting transfers between devices  50 us (43%)
  waiting for transfers between devices  39.9 us (34%)
  blocking collectives  13.4 us (11%)
  Pallas kernels  9.37 us (8%)
  local copies, waits for them, and re-layouts  2.76 us (2%)
    all_to_all x1, waiting for transfers between devices, local(): lax.all_to_all(packed.transpose(1, 0, 2), 'z', 0, 0).transpose(1, 0, 2)  25.4 us
    all_to_all x1, starting transfers between devices, local(): lax.all_to_all(packed.transpose(1, 0, 2), 'z', 0, 0).transpose(1, 0, 2)  21 us
    ppermute x1, starting transfers between devices, local(): got = lax.ppermute(other, 'core', swap)  16.1 us
    all_to_all x1, blocking collectives, local(): own = lax.all_to_all(sent, XY, 0, 0)  13.4 us
    all_to_all x1, waiting for transfers between devices, local(): plane = lax.all_to_all(chip, XY, 0, 0)  12.2 us
    ppermute x1, starting transfers between devices, local(): far = lax.ppermute(own, 'core', swap)  7.29 us
    all_to_all x1, starting transfers between devices, local(): plane = lax.all_to_all(chip, XY, 0, 0)  3.74 us
    pallas_call x1, Pallas kernels, local(): call(functools.partial(far_body, taps, depth), (shape((length, width), BF...  2.97 us
  transfers between devices with their start and end apart: 5, of which 3 were waited for; matrix products, arithmetic and copies ran while one was open for 0% of the time, Pallas kernels for 3%

profile of v6, /device:TPU:1, one launch (start us, length us, event | category | flops | bytes accessed | tf_op | source)
XLA Modules:
  0.0 116.3 jit_solution(14230632554978779029)
XLA Ops:
  0.6 0.0 copy-start
  0.6 1.0 copy-done
  1.6 0.0 copy-start.2
  1.6 1.0 copy-done.2
  2.6 1.2 %shard_map.58 = (bf16[16,64,384]{2,1,0:T(8,128)(2,1)S(1)}, bf16[512,384]{1,0:T(8,128)(2,1)S(1)}, bf16[384,512]{1,0:T(8,128)(2,1)S(1)}, bf16[4,384]{1,0:T(4,128)(...) custom-call(s32[1]{0:T(128)} %bitcast.core_ref, bf16[512,384]{1,0:T(8,128)(2,1)S(1)} %bitcast.17, ...), custom_call_target="tpu_custom_call" | custom-call | flops 528482304 | bytes 3145728 | tf_op jit(solution)/shard_map/pallas_call | solution.py:339
  3.9 16.1 %collective-permute-start = (bf16[16,64,384]{2,1,0:T(8,128)(2,1)S(1)}, bf16[16,64,384]{2,1,0:T(8,128)(2,1)S(1)}, u32[]{:S(2)}, u32[]{:S(2)}) collective-permute-start(bf16[16,64,384]{2,1,0:T(8,128)(2,1)S(1)} %get-tuple-element.22), channel_id=1, source_target_pairs={{0,1},{1,0},{2,3},{3,2},{4,5},{5,4},{6,7},{7,6},{8,9},{9,8},{10,11... | collective-permute-start | bytes 2359304 | tf_op jit(solution)/shard_map/ppermute | solution.py:355
  19.9 1.9 %collective-permute-start.1 = (bf16[4,384]{1,0:T(4,128)(2,1)S(1)}, bf16[4,384]{1,0:T(4,128)(2,1)S(1)}, u32[]{:S(2)}, u32[]{:S(2)}) collective-permute-start(bf16[4,384]{1,0:T(4,128)(2,1)S(1)} %get-tuple-element.23), channel_id=1, source_target_pairs={{1,2},{3,4},{5,6},{7,8},{9,10},{11,12},{13,14},{15,16},{17,18},{19... | collective-permute-start | bytes 9224 | tf_op jit(solution)/shard_map/ppermute | solution.py:357
  21.9 0.7 shard_map.59.mine_ref
  22.6 2.3 %collective-permute-done.1.outer_ref = bf16[4,384]{1,0:T(4,128)(2,1)S(1)} collective-permute-done((bf16[4,384]{1,0:T(4,128)(2,1)S(1)}, bf16[4,384]{1,0:T(4,128)(2,1)S(1)}, u32[]{:S(2)}, u32[]{:S(2)}) %collective-permute-start.1) | collective-permute-done | bytes 3104 | tf_op jit(solution)/shard_map/ppermute | solution.py:357
  24.9 0.0 collective-permute-done.got_ref
  24.9 0.0 copy-start.4
  24.9 1.4 %shard_map.60 = (bf16[16,64,384]{2,1,0:T(8,128)(2,1)}, bf16[4,384]{1,0:T(4,128)(2,1)S(1)}, bf16[4,384]{1,0:T(4,128)(2,1)S(1)}) custom-call(s32[1]{0:T(128)} %bitcast.core_ref, f32[15,64,384]{2,1,0:T(8,128)S(1)} %shard_map.59.mine_ref, bf16[16,64,384]{2,1,0:T(8,128)(2,1)S(1)} %collective-permute-done.got_ref, ...), custom_call_target="tpu_custom_call" | custom-call | flops 368640 | bytes 2949120 | tf_op jit(solution)/shard_map/pallas_call | solution.py:367
  26.2 0.0 copy-start.1
  26.2 0.0 copy-start.3
  26.2 3.7 %all-to-all-start = ((bf16[16,64,384]{2,1,0:T(8,128)(2,1)}), bf16[16,64,384]{2,1,0:T(8,128)(2,1)S(1)}, u32[]{:S(2)}, u32[]{:S(2)}) async-start(bf16[16,64,384]{2,1,0:T(8,128)(2,1)} %get-tuple-element.28), calls=%async_computation | async-start | bytes 1572864 | tf_op jit(solution)/shard_map/all_to_all | solution.py:375
  30.0 0.0 copy-done.4
  30.1 12.2 %all-to-all-done.plane_ref = bf16[16,64,384]{2,1,0:T(8,128)(2,1)S(1)} async-done(((bf16[16,64,384]{2,1,0:T(8,128)(2,1)}), bf16[16,64,384]{2,1,0:T(8,128)(2,1)S(1)}, u32[]{:S(2)}, u32[]{:S(2)}) %all-to-all-start) | async-done | bytes 786464 | tf_op jit(solution)/shard_map/all_to_all | solution.py:375
  42.3 0.1 shard_map.61.packed_ref
  42.4 0.7 copy.6
  43.1 21.0 %all-to-all-start.1 = ((bf16[32,4,384]{2,1,0:T(4,128)(2,1)}), bf16[32,4,384]{2,1,0:T(4,128)(2,1)S(1)}, u32[]{:S(2)}, u32[]{:S(2)}) async-start(bf16[32,4,384]{2,1,0:T(4,128)(2,1)} %copy.6), calls=%async_computation.1 | async-start | bytes 196608 | tf_op jit(solution)/shard_map/all_to_all | solution.py:396
  64.2 0.0 copy-done.1
  64.2 0.0 copy-done.3
  64.2 0.9 shard_map.62
  65.1 25.4 %all-to-all-done.1 = bf16[32,4,384]{2,1,0:T(4,128)(2,1)S(1)} async-done(((bf16[32,4,384]{2,1,0:T(4,128)(2,1)}), bf16[32,4,384]{2,1,0:T(4,128)(2,1)S(1)}, u32[]{:S(2)}, u32[]{:S(2)}) %all-to-all-start.1) | async-done | bytes 98336 | tf_op jit(solution)/shard_map/all_to_all | solution.py:396
  90.5 0.1 shard_map.63
  90.6 13.4 %all_to_all.15.own_ref = bf16[16,72,384]{2,1,0:T(8,128)(2,1)S(1)} all-to-all(bf16[16,72,384]{2,1,0:T(8,128)(2,1)S(1)} %shard_map.63), channel_id=1, replica_groups=mesh['x'=4,'y'=4,'z'=32,'core'=2] {'x','y'}, dimensions={0} | all-to-all | bytes 1769472 | tf_op jit(solution)/shard_map/all_to_all | solution.py:406
  104.0 7.3 %collective-permute-start.2 = (bf16[16,72,384]{2,1,0:T(8,128)(2,1)S(1)}, bf16[16,72,384]{2,1,0:T(8,128)(2,1)S(1)}, u32[]{:S(2)}, u32[]{:S(2)}) collective-permute-start(bf16[16,72,384]{2,1,0:T(8,128)(2,1)S(1)} %all_to_all.15.own_ref), channel_id=1, source_target_pairs={{0,1},{1,0},{2,3},{3,2},{4,5},{5,4},{6,7},{7,6},{8,9},{9,8},{10,11... | collective-permute-start | bytes 2654216 | tf_op jit(solution)/shard_map/ppermute | solution.py:407
  111.3 2.0 %shard_map.64 = (bf16[512,192]{1,0:T(8,128)(2,1)S(1)}, f32[512,384]{1,0:T(8,128)S(1)}, f32[5,6,384]{2,1,0:T(8,128)}) custom-call(bf16[528,384]{1,0:T(8,128)(2,1)S(1)} %get-tuple-element.30.after_ref.act_ref, bf16[528,384]{1,0:T(8,128)(2,1)S(1)} %get-tuple-element.31.cot_ref, bf16[16,72,384]{2,1,0:T(8,128)(2,1)S(1)} %all_to_all.15.own_ref), custom_call_target="tpu_custom_call" | custom-call | flops 754974720 | bytes 3145728 | tf_op jit(solution)/shard_map/pallas_call | solution.py:409
  113.3 0.0 collective-permute-done.2.far_ref
  113.3 3.0 %shard_map.65 = (bf16[512,384]{1,0:T(8,128)(2,1)}, bf16[512,384]{1,0:T(8,128)(2,1)}) custom-call(s32[1]{0:T(128)} %bitcast.core_ref, bf16[512,384]{1,0:T(8,128)(2,1)S(1)} %bitcast.19, bf16[512,384]{1,0:T(8,128)(2,1)S(1)} %bitcast.22, f32[512,384]{1,0:T(8,128)S(1)} %get-tuple-element.29.slope_ref, bf16[512,192]{1,0:T(8,128)(2,1)S(1)} %get-tuple-element.32.near_ref, ...), custom_call_target="tpu_custom_call" | custom-call | flops 754974720 | bytes 4718592 | tf_op jit(solution)/shard_map/pallas_call | solution.py:422
  (3 shorter events, 0.1 us)
Async XLA Ops:
  0.6 1.0 copy-start
  1.6 1.0 copy-start.2
  3.9 21.0 %collective-permute-start = (bf16[16,64,384]{2,1,0:T(8,128)(2,1)S(1)}, bf16[16,64,384]{2,1,0:T(8,128)(2,1)S(1)}, u32[]{:S(2)}, u32[]{:S(2)}) collective-permute-start(bf16[16,64,384]{2,1,0:T(8,128)(2,1)S(1)} %get-tuple-element.22), channel_id=1, source_target_pairs={{0,1},{1,0},{2,3},{3,2},{4,5},{5,4},{6,7},{7,6},{8,9},{9,8},{10,11... | collective-permute-start | bytes 2359304 | tf_op jit(solution)/shard_map/ppermute | solution.py:355
  19.9 4.9 %collective-permute-start.1 = (bf16[4,384]{1,0:T(4,128)(2,1)S(1)}, bf16[4,384]{1,0:T(4,128)(2,1)S(1)}, u32[]{:S(2)}, u32[]{:S(2)}) collective-permute-start(bf16[4,384]{1,0:T(4,128)(2,1)S(1)} %get-tuple-element.23), channel_id=1, source_target_pairs={{1,2},{3,4},{5,6},{7,8},{9,10},{11,12},{13,14},{15,16},{17,18},{19... | collective-permute-start | bytes 9224 | tf_op jit(solution)/shard_map/ppermute | solution.py:357
  24.9 5.1 %copy-start.4 = (bf16[6,5,384]{2,0,1:T(8,128)(2,1)S(1)}, bf16[6,5,384]{2,0,1:T(8,128)(2,1)}, u32[]{:S(2)}) copy-start(bf16[6,5,384]{2,0,1:T(8,128)(2,1)} %param.4) | copy-start | bytes 69124
  26.2 37.9 %copy-start.1 = (bf16[1,512,384]{2,1,0:T(8,128)(2,1)S(1)}, bf16[1,512,384]{2,1,0:T(8,128)(2,1)}, u32[]{:S(2)}) copy-start(bf16[1,512,384]{2,1,0:T(8,128)(2,1)} %param.3) | copy-start | bytes 1179652
  26.2 37.9 %copy-start.3 = (bf16[1,512,384]{2,1,0:T(8,128)(2,1)S(1)}, bf16[1,512,384]{2,1,0:T(8,128)(2,1)}, u32[]{:S(2)}) copy-start(bf16[1,512,384]{2,1,0:T(8,128)(2,1)} %param.5) | copy-start | bytes 1179652
  26.2 16.1 %all-to-all-start = ((bf16[16,64,384]{2,1,0:T(8,128)(2,1)}), bf16[16,64,384]{2,1,0:T(8,128)(2,1)S(1)}, u32[]{:S(2)}, u32[]{:S(2)}) async-start(bf16[16,64,384]{2,1,0:T(8,128)(2,1)} %get-tuple-element.28), calls=%async_computation | async-start | bytes 1572864 | tf_op jit(solution)/shard_map/all_to_all | solution.py:375
  43.1 47.3 %all-to-all-start.1 = ((bf16[32,4,384]{2,1,0:T(4,128)(2,1)}), bf16[32,4,384]{2,1,0:T(4,128)(2,1)S(1)}, u32[]{:S(2)}, u32[]{:S(2)}) async-start(bf16[32,4,384]{2,1,0:T(4,128)(2,1)} %copy.6), calls=%async_computation.1 | async-start | bytes 196608 | tf_op jit(solution)/shard_map/all_to_all | solution.py:396
  104.0 9.3 %collective-permute-start.2 = (bf16[16,72,384]{2,1,0:T(8,128)(2,1)S(1)}, bf16[16,72,384]{2,1,0:T(8,128)(2,1)S(1)}, u32[]{:S(2)}, u32[]{:S(2)}) collective-permute-start(bf16[16,72,384]{2,1,0:T(8,128)(2,1)S(1)} %all_to_all.15.own_ref), channel_id=1, source_target_pairs={{0,1},{1,0},{2,3},{3,2},{4,5},{5,4},{6,7},{7,6},{8,9},{9,8},{10,11... | collective-permute-start | bytes 2654216 | tf_op jit(solution)/shard_map/ppermute | solution.py:407

commit v7 on v6

--- a/solution.py
+++ b/solution.py
@@ -177,10 +177,11 @@
     for i in range(1, plane_ref.shape[0]):
         total = total + plane_ref[i].astype(F32)
     rows = row_ref[...].astype(F32)
-    out_ref[0] = jnp.broadcast_to(rows[0:1], out_ref.shape[1:]).astype(BF)
-    out_ref[1] = jnp.broadcast_to(rows[1:2], out_ref.shape[1:]).astype(BF)
-    out_ref[2] = total[:depth].astype(BF)
-    out_ref[3] = total[depth:].astype(BF)
+    width = rows.shape[1]
+    row_pair = rows.astype(BF).reshape(1, 2, width)
+    parts = total.reshape(2, depth, width)
+    pair = jnp.stack([parts[0], parts[1]], axis=1).astype(BF)
+    out_ref[...] = jnp.concatenate([jnp.broadcast_to(row_pair, (depth, 2, width)), pair], axis=1)
 
 
 def line_body(share, line_ref, after_ref, out_ref):
@@ -378,7 +379,7 @@
     rows = lax.dynamic_index_in_dim(by_block, jnp.minimum(spot, blocks - 1), 0, keepdims=False)
     packed = call(
         functools.partial(plane_body, depth),
-        shape((4, depth, width), BF),
+        shape((depth, 4, width), BF),
         groups * 2 * depth * width,
         groups * 2 * depth * width * 2,
         0,
@@ -393,7 +394,7 @@
         4,
         far=1,
     )(core, x, g, before, after, packed)
-    line = lax.all_to_all(packed.transpose(1, 0, 2), "z", 0, 0).transpose(1, 0, 2)
+    line = lax.all_to_all(packed, "z", 0, 0).transpose(1, 0, 2)
     sent = call(
         functools.partial(line_body, float(groups * section_input.shape[0])),
         shape((groups, 2 * depth + 8, width), BF),

time: 117 us -> 117 us (level)
  no operation moved by 1% of the time
where the time goes in v7:
time: 117 us; the launch traced here: 116 us
  starting transfers between devices  50 us (43%)
  waiting for transfers between devices  39.9 us (34%)
  blocking collectives  13.4 us (11%)
  Pallas kernels  10.1 us (9%)
  local copies, waits for them, and re-layouts  2.06 us (2%)
    all_to_all x1, waiting for transfers between devices, local(): line = lax.all_to_all(packed, 'z', 0, 0).transpose(1, 0, 2)  25.4 us
    all_to_all x1, starting transfers between devices, local(): line = lax.all_to_all(packed, 'z', 0, 0).transpose(1, 0, 2)  21 us
    ppermute x1, starting transfers between devices, local(): got = lax.ppermute(other, 'core', swap)  16.1 us
    all_to_all x1, blocking collectives, local(): own = lax.all_to_all(sent, XY, 0, 0)  13.4 us
    all_to_all x1, waiting for transfers between devices, local(): plane = lax.all_to_all(chip, XY, 0, 0)  12.2 us
    ppermute x1, starting transfers between devices, local(): far = lax.ppermute(own, 'core', swap)  7.29 us
    all_to_all x1, starting transfers between devices, local(): plane = lax.all_to_all(chip, XY, 0, 0)  3.74 us
    pallas_call x1, Pallas kernels, local(): call(functools.partial(far_body, taps, depth), (shape((length, width), BF...  2.97 us
  transfers between devices with their start and end apart: 5, of which 3 were waited for; matrix products, arithmetic and copies ran while one was open for 0% of the time, Pallas kernels for 3%

profile of v7, /device:TPU:1, one launch (start us, length us, event | category | flops | bytes accessed | tf_op | source)
XLA Modules:
  0.0 116.3 jit_solution(12613640480202874721)
XLA Ops:
  0.6 0.0 copy-start
  0.6 1.0 copy-done
  1.6 0.0 copy-start.2
  1.6 1.0 copy-done.2
  2.6 1.2 %shard_map.58 = (bf16[16,64,384]{2,1,0:T(8,128)(2,1)S(1)}, bf16[512,384]{1,0:T(8,128)(2,1)S(1)}, bf16[384,512]{1,0:T(8,128)(2,1)S(1)}, bf16[4,384]{1,0:T(4,128)(...) custom-call(s32[1]{0:T(128)} %bitcast.core_ref, bf16[512,384]{1,0:T(8,128)(2,1)S(1)} %bitcast.16, ...), custom_call_target="tpu_custom_call" | custom-call | flops 528482304 | bytes 3145728 | tf_op jit(solution)/shard_map/pallas_call | solution.py:340
  3.9 16.1 %collective-permute-start = (bf16[16,64,384]{2,1,0:T(8,128)(2,1)S(1)}, bf16[16,64,384]{2,1,0:T(8,128)(2,1)S(1)}, u32[]{:S(2)}, u32[]{:S(2)}) collective-permute-start(bf16[16,64,384]{2,1,0:T(8,128)(2,1)S(1)} %get-tuple-element.22), channel_id=1, source_target_pairs={{0,1},{1,0},{2,3},{3,2},{4,5},{5,4},{6,7},{7,6},{8,9},{9,8},{10,11... | collective-permute-start | bytes 2359304 | tf_op jit(solution)/shard_map/ppermute | solution.py:356
  19.9 1.9 %collective-permute-start.1 = (bf16[4,384]{1,0:T(4,128)(2,1)S(1)}, bf16[4,384]{1,0:T(4,128)(2,1)S(1)}, u32[]{:S(2)}, u32[]{:S(2)}) collective-permute-start(bf16[4,384]{1,0:T(4,128)(2,1)S(1)} %get-tuple-element.23), channel_id=1, source_target_pairs={{1,2},{3,4},{5,6},{7,8},{9,10},{11,12},{13,14},{15,16},{17,18},{19... | collective-permute-start | bytes 9224 | tf_op jit(solution)/shard_map/ppermute | solution.py:358
  21.9 0.7 shard_map.59.mine_ref
  22.6 2.3 %collective-permute-done.1.outer_ref = bf16[4,384]{1,0:T(4,128)(2,1)S(1)} collective-permute-done((bf16[4,384]{1,0:T(4,128)(2,1)S(1)}, bf16[4,384]{1,0:T(4,128)(2,1)S(1)}, u32[]{:S(2)}, u32[]{:S(2)}) %collective-permute-start.1) | collective-permute-done | bytes 3104 | tf_op jit(solution)/shard_map/ppermute | solution.py:358
  24.9 0.0 collective-permute-done.got_ref
  24.9 0.0 copy-start.4
  24.9 1.4 %shard_map.60 = (bf16[16,64,384]{2,1,0:T(8,128)(2,1)}, bf16[4,384]{1,0:T(4,128)(2,1)S(1)}, bf16[4,384]{1,0:T(4,128)(2,1)S(1)}) custom-call(s32[1]{0:T(128)} %bitcast.core_ref, f32[15,64,384]{2,1,0:T(8,128)S(1)} %shard_map.59.mine_ref, bf16[16,64,384]{2,1,0:T(8,128)(2,1)S(1)} %collective-permute-done.got_ref, ...), custom_call_target="tpu_custom_call" | custom-call | flops 368640 | bytes 2949120 | tf_op jit(solution)/shard_map/pallas_call | solution.py:368
  26.2 0.0 copy-start.1
  26.2 0.0 copy-start.3
  26.2 3.7 %all-to-all-start = ((bf16[16,64,384]{2,1,0:T(8,128)(2,1)}), bf16[16,64,384]{2,1,0:T(8,128)(2,1)S(1)}, u32[]{:S(2)}, u32[]{:S(2)}) async-start(bf16[16,64,384]{2,1,0:T(8,128)(2,1)} %get-tuple-element.28), calls=%async_computation | async-start | bytes 1572864 | tf_op jit(solution)/shard_map/all_to_all | solution.py:376
  30.0 0.0 copy-done.4
  30.1 12.2 %all-to-all-done.plane_ref = bf16[16,64,384]{2,1,0:T(8,128)(2,1)S(1)} async-done(((bf16[16,64,384]{2,1,0:T(8,128)(2,1)}), bf16[16,64,384]{2,1,0:T(8,128)(2,1)S(1)}, u32[]{:S(2)}, u32[]{:S(2)}) %all-to-all-start) | async-done | bytes 786464 | tf_op jit(solution)/shard_map/all_to_all | solution.py:376
  42.3 0.9 shard_map.61.packed_ref
  43.2 21.0 %all-to-all-start.1 = ((bf16[32,4,384]{2,1,0:T(4,128)(2,1)}), bf16[32,4,384]{2,1,0:T(4,128)(2,1)S(1)}, u32[]{:S(2)}, u32[]{:S(2)}) async-start(bf16[32,4,384]{2,1,0:T(4,128)(2,1)} %shard_map.61.packed_ref), calls=%async_computation.1 | async-start | bytes 196608 | tf_op jit(solution)/shard_map/all_to_all | solution.py:397
  64.2 0.0 copy-done.1
  64.2 0.0 copy-done.3
  64.2 0.9 shard_map.62
  65.1 25.4 %all-to-all-done.1 = bf16[32,4,384]{2,1,0:T(4,128)(2,1)S(1)} async-done(((bf16[32,4,384]{2,1,0:T(4,128)(2,1)}), bf16[32,4,384]{2,1,0:T(4,128)(2,1)S(1)}, u32[]{:S(2)}, u32[]{:S(2)}) %all-to-all-start.1) | async-done | bytes 98336 | tf_op jit(solution)/shard_map/all_to_all | solution.py:397
  90.5 0.1 shard_map.63
  90.6 13.4 %all_to_all.15.own_ref = bf16[16,72,384]{2,1,0:T(8,128)(2,1)S(1)} all-to-all(bf16[16,72,384]{2,1,0:T(8,128)(2,1)S(1)} %shard_map.63), channel_id=1, replica_groups=mesh['x'=4,'y'=4,'z'=32,'core'=2] {'x','y'}, dimensions={0} | all-to-all | bytes 1769472 | tf_op jit(solution)/shard_map/all_to_all | solution.py:407
  104.0 7.3 %collective-permute-start.2 = (bf16[16,72,384]{2,1,0:T(8,128)(2,1)S(1)}, bf16[16,72,384]{2,1,0:T(8,128)(2,1)S(1)}, u32[]{:S(2)}, u32[]{:S(2)}) collective-permute-start(bf16[16,72,384]{2,1,0:T(8,128)(2,1)S(1)} %all_to_all.15.own_ref), channel_id=1, source_target_pairs={{0,1},{1,0},{2,3},{3,2},{4,5},{5,4},{6,7},{7,6},{8,9},{9,8},{10,11... | collective-permute-start | bytes 2654216 | tf_op jit(solution)/shard_map/ppermute | solution.py:408
  111.3 2.0 %shard_map.64 = (bf16[512,192]{1,0:T(8,128)(2,1)S(1)}, f32[512,384]{1,0:T(8,128)S(1)}, f32[5,6,384]{2,1,0:T(8,128)}) custom-call(bf16[528,384]{1,0:T(8,128)(2,1)S(1)} %get-tuple-element.30.after_ref.act_ref, bf16[528,384]{1,0:T(8,128)(2,1)S(1)} %get-tuple-element.31.cot_ref, bf16[16,72,384]{2,1,0:T(8,128)(2,1)S(1)} %all_to_all.15.own_ref), custom_call_target="tpu_custom_call" | custom-call | flops 754974720 | bytes 3145728 | tf_op jit(solution)/shard_map/pallas_call | solution.py:410
  113.3 0.0 collective-permute-done.2.far_ref
  113.4 3.0 %shard_map.65 = (bf16[512,384]{1,0:T(8,128)(2,1)}, bf16[512,384]{1,0:T(8,128)(2,1)}) custom-call(s32[1]{0:T(128)} %bitcast.core_ref, bf16[512,384]{1,0:T(8,128)(2,1)S(1)} %bitcast.18, bf16[512,384]{1,0:T(8,128)(2,1)S(1)} %bitcast.21, f32[512,384]{1,0:T(8,128)S(1)} %get-tuple-element.29.slope_ref, bf16[512,192]{1,0:T(8,128)(2,1)S(1)} %get-tuple-element.32.near_ref, ...), custom_call_target="tpu_custom_call" | custom-call | flops 754974720 | bytes 4718592 | tf_op jit(solution)/shard_map/pallas_call | solution.py:423
  (3 shorter events, 0.1 us)
Async XLA Ops:
  0.6 1.0 copy-start
  1.6 1.0 copy-start.2
  3.9 21.0 %collective-permute-start = (bf16[16,64,384]{2,1,0:T(8,128)(2,1)S(1)}, bf16[16,64,384]{2,1,0:T(8,128)(2,1)S(1)}, u32[]{:S(2)}, u32[]{:S(2)}) collective-permute-start(bf16[16,64,384]{2,1,0:T(8,128)(2,1)S(1)} %get-tuple-element.22), channel_id=1, source_target_pairs={{0,1},{1,0},{2,3},{3,2},{4,5},{5,4},{6,7},{7,6},{8,9},{9,8},{10,11... | collective-permute-start | bytes 2359304 | tf_op jit(solution)/shard_map/ppermute | solution.py:356
  19.9 4.9 %collective-permute-start.1 = (bf16[4,384]{1,0:T(4,128)(2,1)S(1)}, bf16[4,384]{1,0:T(4,128)(2,1)S(1)}, u32[]{:S(2)}, u32[]{:S(2)}) collective-permute-start(bf16[4,384]{1,0:T(4,128)(2,1)S(1)} %get-tuple-element.23), channel_id=1, source_target_pairs={{1,2},{3,4},{5,6},{7,8},{9,10},{11,12},{13,14},{15,16},{17,18},{19... | collective-permute-start | bytes 9224 | tf_op jit(solution)/shard_map/ppermute | solution.py:358
  24.9 5.1 %copy-start.4 = (bf16[6,5,384]{2,0,1:T(8,128)(2,1)S(1)}, bf16[6,5,384]{2,0,1:T(8,128)(2,1)}, u32[]{:S(2)}) copy-start(bf16[6,5,384]{2,0,1:T(8,128)(2,1)} %param.4) | copy-start | bytes 69124
  26.2 38.0 %copy-start.1 = (bf16[1,512,384]{2,1,0:T(8,128)(2,1)S(1)}, bf16[1,512,384]{2,1,0:T(8,128)(2,1)}, u32[]{:S(2)}) copy-start(bf16[1,512,384]{2,1,0:T(8,128)(2,1)} %param.3) | copy-start | bytes 1179652
  26.2 38.0 %copy-start.3 = (bf16[1,512,384]{2,1,0:T(8,128)(2,1)S(1)}, bf16[1,512,384]{2,1,0:T(8,128)(2,1)}, u32[]{:S(2)}) copy-start(bf16[1,512,384]{2,1,0:T(8,128)(2,1)} %param.5) | copy-start | bytes 1179652
  26.2 16.1 %all-to-all-start = ((bf16[16,64,384]{2,1,0:T(8,128)(2,1)}), bf16[16,64,384]{2,1,0:T(8,128)(2,1)S(1)}, u32[]{:S(2)}, u32[]{:S(2)}) async-start(bf16[16,64,384]{2,1,0:T(8,128)(2,1)} %get-tuple-element.28), calls=%async_computation | async-start | bytes 1572864 | tf_op jit(solution)/shard_map/all_to_all | solution.py:376
  43.2 47.3 %all-to-all-start.1 = ((bf16[32,4,384]{2,1,0:T(4,128)(2,1)}), bf16[32,4,384]{2,1,0:T(4,128)(2,1)S(1)}, u32[]{:S(2)}, u32[]{:S(2)}) async-start(bf16[32,4,384]{2,1,0:T(4,128)(2,1)} %shard_map.61.packed_ref), calls=%async_computation.1 | async-start | bytes 196608 | tf_op jit(solution)/shard_map/all_to_all | solution.py:397
  104.0 9.3 %collective-permute-start.2 = (bf16[16,72,384]{2,1,0:T(8,128)(2,1)S(1)}, bf16[16,72,384]{2,1,0:T(8,128)(2,1)S(1)}, u32[]{:S(2)}, u32[]{:S(2)}) collective-permute-start(bf16[16,72,384]{2,1,0:T(8,128)(2,1)S(1)} %all_to_all.15.own_ref), channel_id=1, source_target_pairs={{0,1},{1,0},{2,3},{3,2},{4,5},{5,4},{6,7},{7,6},{8,9},{9,8},{10,11... | collective-permute-start | bytes 2654216 | tf_op jit(solution)/shard_map/ppermute | solution.py:408
